TPU v7x, 32 devices: a whole 2x2x4 slice. The times are simulated.
32 devices in a mesh: groups: 2 (over y), blk: 8 (over z, x), tensor: 2 (over core).
Axes of the slice: x: 2, y: 2, z: 4, core: 2. Of those that a mesh axis runs over, the one named last changes fastest.
Arguments:
- hidden: bfloat16 [128, 64, 4096], P(('groups', 'blk'), None, 'tensor'), parts along dimension 0
- cotangent: bfloat16 [128, 64, 4096], P(('groups', 'blk'), None, 'tensor'), parts along dimension 0
- token_loss_mask: int32 [128, 64], P(('groups', 'blk')), parts along dimension 0, may hold values 0 or 1
- adapter_down_factor: bfloat16 [16, 4096], P(None, 'tensor'), may hold values from -0.09375 to 0.09375
- adapter_up_factor: bfloat16 [4096, 16], P('tensor'), may hold values from -0.09375 to 0.09375
- sign_table_salts: int32 [4], replicated, may hold values from 0 to 1048575
Outputs:
- kernel: float32 [128, 64], P(('groups', 'blk', 'tensor')), parts along dimension 0
There are 2 independent parts, one for each index of `groups`. A program takes and returns all parts, laid end to end along the dimension named above; an argument that names none is the same for every part. Nothing has to cross between parts.
All inputs are finite; a program needn't handle non-finite values. No bound on the sum of `token_loss_mask` on one device may be relied on, other than what follows from the above.
Results may differ from a plain program's by a relative error of at most 0.00035.
Values may be sent and summed in bfloat16 or wider, within the bound.
No kernel may reach another device: no remote copies, remote signals or barrier semaphores. Data moves between devices by JAX's collectives and lax.ppermute only.
A program may use at most 64 MiB of HBM per device.

v0:
```python
import functools
import math

import jax
import jax.numpy as jnp
from jax import lax
from jax.experimental import pallas as pl
from jax.experimental.pallas import tpu as pltpu
from jax.sharding import Mesh, PartitionSpec as P

MODEL_WIDTH = 4096
ADAPTER_RANK = 16
PROJ_ROWS = 256
SEQ = 64
SCALE = 1.0 / math.sqrt(PROJ_ROWS * ADAPTER_RANK * ADAPTER_RANK * SEQ * MODEL_WIDTH)
PIECES = 3
LANES = 128
BLOCK = (16, 256)
BLK = ("z", "x")

F32 = jnp.float32
BF16 = jnp.bfloat16
I32 = jnp.int32
NT = (((1,), (1,)), ((), ()))
VMEM = pl.BlockSpec(memory_space=pltpu.VMEM)
SMEM = pl.BlockSpec(memory_space=pltpu.SMEM)
HBM = pl.BlockSpec(memory_space=pltpu.HBM)
SMALL = pltpu.CompilerParams(vmem_limit_bytes=16 * 1024 * 1024)

INDEX_MUL = -1640531535
SALT_MUL = 668265263


def int32_wrap(value):
    return (value + 2**31) % 2**32 - 2**31


def hash_sign(hashed):
    hashed = hashed ^ lax.shift_right_logical(hashed, 15)
    hashed = hashed * -2048144789
    hashed = hashed ^ lax.shift_right_logical(hashed, 13)
    hashed = hashed * int32_wrap(-1028477387 << 6)
    hashed = hashed ^ lax.shift_left(hashed, 16)
    return jnp.where(hashed < 0, 1.0, -1.0).astype(F32)


def iota(shape, dim):
    return lax.broadcasted_iota(I32, shape, dim)


def token_row(mask):
    ex_rows, seq = mask.shape
    tokens = ex_rows * seq
    tiled = jnp.concatenate([mask.astype(F32)] * ex_rows, axis=1)
    owner = iota((ex_rows, tokens), 1) // seq == iota((ex_rows, tokens), 0)
    return jnp.sum(jnp.where(owner, tiled, 0.0), axis=0, keepdims=True)


def split_pieces(value):
    pieces = []
    for _ in range(PIECES):
        pieces.append(value.astype(BF16))
        value = value - pieces[-1].astype(F32)
    return jnp.concatenate(pieces, axis=0)


def kind_of(cross):
    core = lax.axis_index("tensor")
    return core ^ (lax.axis_index("z") // (lax.axis_size("z") // 2)) if cross else core


def table_start():
    index = iota(BLOCK, 1) * PROJ_ROWS + iota(BLOCK, 0)
    return index * INDEX_MUL


def sign_rows(start, col):
    high, wide = BLOCK
    rows = [
        hash_sign(start + int32_wrap((col * PROJ_ROWS + row) * INDEX_MUL)).astype(BF16)
        for row in range(0, PROJ_ROWS, high)
    ]
    return rows


def far_kernel(
    cross, ex_rows,
    salts_hbm, mask_hbm, down_hbm, up_hbm, hid_hbm, cot_hbm,
    send_ref, ranks_ref, near_ref, start_ref, kept_ref, mixer_ref,
    salts, mask, far_factor, near_factor, far, sems,
):
    tokens, width = far.shape
    kind = kind_of(cross)
    parts = 4
    share = width // parts
    wide = BLOCK[1]

    def copies(inputs, factor, factor_held, held, first):
        out = [pltpu.make_async_copy(factor, factor_held, sems.at[first])]
        for i in range(parts):
            cols = pl.ds(i * share, share)
            out.append(
                pltpu.make_async_copy(inputs.at[:, cols], held.at[:, cols], sems.at[first + 1 + i])
            )
        return out

    def start_copies(far_inputs, far_part, near_inputs, near_part):
        far_copies = copies(far_inputs, far_part, far_factor, far, 2)
        near_copies = copies(near_inputs, near_part, near_factor, near_ref, parts + 3)
        for pair in zip(far_copies, near_copies):
            for copy in pair:
                copy.start()

    salts_copy = pltpu.make_async_copy(salts_hbm, salts, sems.at[0])
    mask_copy = pltpu.make_async_copy(mask_hbm, mask, sems.at[1])
    salts_copy.start()

    @pl.when(kind == 0)
    def _():
        start_copies(hid_hbm, down_hbm, cot_hbm, up_hbm)

    @pl.when(kind == 1)
    def _():
        start_copies(cot_hbm, up_hbm, hid_hbm, down_hbm)

    mask_copy.start()
    far_waits = copies(hid_hbm, down_hbm, far_factor, far, 2)
    near_waits = copies(hid_hbm, down_hbm, near_factor, near_ref, parts + 3)
    first = lax.axis_index("tensor") * int32_wrap(width * PROJ_ROWS * INDEX_MUL)
    start = table_start() + first
    salts_copy.wait()
    far_start = start + salts[2 - 2 * kind] * SALT_MUL
    far_waits[0].wait()
    near_waits[0].wait()
    total = ranks = None
    for col in range(0, width, wide):
        part = slice(col, col + wide)
        left = jnp.concatenate(sign_rows(far_start, col) + [far_factor[:, part]], axis=0)
        if col % share == 0:
            far_waits[1 + col // share].wait()
            near_waits[1 + col // share].wait()
        term = lax.dot_general(left, far[:, part], NT, preferred_element_type=F32)
        total = term if total is None else total + term
        term = lax.dot_general(
            near_factor[:, part], near_ref[:, part], NT, preferred_element_type=F32
        )
        ranks = term if ranks is None else ranks + term
    start_ref[...] = start + salts[2 * kind] * SALT_MUL
    shape = mixer_ref.shape
    mixed, rank = iota(shape, 0) // ex_rows, iota(shape, 1) % ADAPTER_RANK
    index = (rank * ADAPTER_RANK + mixed) * INDEX_MUL
    mixer_ref[...] = hash_sign(index + salts[1 + 2 * kind] * SALT_MUL).astype(BF16)
    mask_copy.wait()
    counted = token_row(mask[...]) != 0
    far_kept = counted | (kind == 0)
    near_kept = counted | (kind == 1)
    kept_ref[...] = jnp.broadcast_to(jnp.where(near_kept, 1.0, 0.0), kept_ref.shape)
    total = jnp.where(far_kept, total, 0.0)
    send_ref[:PROJ_ROWS] = total[:PROJ_ROWS].astype(BF16)
    ranks_ref[...] = split_pieces(total[PROJ_ROWS:])
    send_ref[PROJ_ROWS:] = split_pieces(jnp.where(near_kept, ranks, 0.0))


def far_rows(salts, mask, down, up, hidden, cotangent, cross):
    ex_rows = mask.shape[0]
    tokens, width = hidden.shape
    pieces = PIECES * ADAPTER_RANK
    arrays = (salts, mask, down, up, hidden, cotangent)
    return pl.pallas_call(
        functools.partial(far_kernel, cross, ex_rows),
        out_shape=[
            jax.ShapeDtypeStruct((PROJ_ROWS + pieces, tokens), BF16),
            jax.ShapeDtypeStruct((pieces, tokens), BF16),
            jax.ShapeDtypeStruct((tokens, width), BF16),
            jax.ShapeDtypeStruct(BLOCK, I32),
            jax.ShapeDtypeStruct((8, tokens), F32),
            jax.ShapeDtypeStruct((ADAPTER_RANK * ex_rows, 2 * pieces), BF16),
        ],
        in_specs=[HBM] * 6,
        out_specs=[VMEM] * 6,
        scratch_shapes=[
            pltpu.SMEM(salts.shape, I32),
            pltpu.VMEM(mask.shape, I32),
            pltpu.VMEM((ADAPTER_RANK, width), BF16),
            pltpu.VMEM((ADAPTER_RANK, width), BF16),
            pltpu.VMEM((tokens, width), BF16),
            pltpu.SemaphoreType.DMA((12,)),
        ],
        compiler_params=SMALL,
    )(*[pltpu.with_memory_space_constraint(x, pltpu.HBM) for x in arrays])


def near_kernel(start_ref, kept_ref, near_ref, out_ref):
    start = start_ref[...]
    wide = BLOCK[1]
    total = None
    for col in range(0, near_ref.shape[1], wide):
        left = jnp.concatenate(sign_rows(start, col), axis=0)
        term = lax.dot_general(
            left, near_ref[:, col : col + wide], NT, preferred_element_type=F32
        )
        total = term if total is None else total + term
    out_ref[...] = jnp.where(kept_ref[:1] != 0, total, 0.0).astype(BF16)


def near_rows(start, kept, near):
    tokens, width = near.shape
    return pl.pallas_call(
        near_kernel,
        out_shape=jax.ShapeDtypeStruct((PROJ_ROWS, tokens), BF16),
        in_specs=[VMEM] * 3,
        out_specs=VMEM,
        compiler_params=SMALL,
        cost_estimate=pl.CostEstimate(
            flops=2 * tokens * width * PROJ_ROWS, bytes_accessed=2 * tokens * width, transcendentals=0
        ),
    )(start, kept, near)


def feature_kernel(ex_rows, mixer_ref, ranks_ref, own_ref, other_ref, out_ref, copies_ref):
    tokens = own_ref.shape[1]
    rows = ADAPTER_RANK * ex_rows
    pieces = jnp.concatenate([ranks_ref[...], other_ref[PROJ_ROWS:]], axis=0)
    coeffs = jnp.dot(mixer_ref[...], pieces, preferred_element_type=F32)
    owned = iota((rows, tokens), 1) // SEQ == iota((rows, tokens), 0) % ex_rows
    coeffs = jnp.where(owned, coeffs, 0.0).astype(BF16)
    projected = lax.dot_general(coeffs, own_ref[...], NT, preferred_element_type=F32)
    projected += lax.dot_general(coeffs, other_ref[:PROJ_ROWS], NT, preferred_element_type=F32)
    features = (projected * SCALE).astype(BF16)
    out_ref[...] = features
    for copy in range(copies_ref.shape[0]):
        copies_ref[copy] = features


def feature_rows(mixer, ranks, own, other, ex_rows, copies):
    rows = ADAPTER_RANK * ex_rows
    return pl.pallas_call(
        functools.partial(feature_kernel, ex_rows),
        out_shape=[
            jax.ShapeDtypeStruct((rows, PROJ_ROWS), BF16),
            jax.ShapeDtypeStruct((copies, rows, PROJ_ROWS), BF16),
        ],
        in_specs=[VMEM] * 4,
        out_specs=[VMEM] * 2,
        compiler_params=SMALL,
    )(mixer, ranks, own, other)


def fold_ranks(terms):
    half = terms.shape[0] // 2
    folded = terms[:half] + pltpu.roll(terms[half:], LANES - half, 1)
    return jnp.where(iota(folded.shape, 1) % (2 * half) < half, folded, 0.0)


def pair_kernel(ex_rows, own_ref, near_ref, got_ref, keep_ref, send_ref):
    blocks, rows, _ = got_ref.shape
    total = None
    for row in range(0, rows, 2 * ex_rows):
        part = slice(row, row + 2 * ex_rows)
        left = jnp.concatenate([own_ref[part, :], near_ref[part, :]], axis=0)
        right = jnp.concatenate([got_ref[b, part, :] for b in range(blocks)] * 2, axis=0)
        term = lax.dot_general(left, right, NT, preferred_element_type=F32)
        total = term if total is None else total + term
    keep_ref[...] = fold_ranks(total[: 2 * ex_rows])
    send_ref[...] = fold_ranks(total[2 * ex_rows :])


def pair_rows(own, near, got, ex_rows):
    return pl.pallas_call(
        functools.partial(pair_kernel, ex_rows),
        out_shape=[jax.ShapeDtypeStruct((ex_rows, LANES), F32)] * 2,
        in_specs=[VMEM] * 3,
        out_specs=[VMEM] * 2,
        compiler_params=SMALL,
    )(own, near, got)


def halves_kernel(own_ref, got_ref, keep_ref, send_ref):
    ex_rows, _ = own_ref.shape
    low_x = lax.axis_index("x") == 0
    first = jnp.where(low_x, own_ref[...], got_ref[...])
    second = jnp.where(low_x, got_ref[...], own_ref[...])
    total = first + pltpu.roll(second, ex_rows, 1)
    half = keep_ref.shape[0]
    low = lax.axis_index("tensor") == 0
    keep_ref[...] = jnp.where(low, total[:half], total[half:])
    send_ref[...] = jnp.where(low, total[half:], total[:half])


def join_halves(own, got):
    rows, lanes = own.shape
    return pl.pallas_call(
        halves_kernel,
        out_shape=[jax.ShapeDtypeStruct((rows // 2, lanes), F32)] * 2,
        in_specs=[VMEM] * 2,
        out_specs=[VMEM] * 2,
        compiler_params=SMALL,
    )(own, got)


def sum_kernel(keep_ref, got_ref, out_ref):
    out_ref[...] = (keep_ref[...] + got_ref[...])[:, : out_ref.shape[1]]


def sum_rows(keep, got):
    return pl.pallas_call(
        sum_kernel,
        out_shape=jax.ShapeDtypeStruct((keep.shape[0], LANES // 2), F32),
        in_specs=[VMEM] * 2,
        out_specs=VMEM,
        compiler_params=SMALL,
    )(keep, got)


def swap_cores(value):
    return lax.ppermute(value, "tensor", [(0, 1), (1, 0)])


def swap_across(value):
    return lax.ppermute(value, ("x", "tensor"), [(i, i ^ 3) for i in range(4)])


def swap_x(value):
    return lax.ppermute(value, "x", [(0, 1), (1, 0)])


def trade_z(parts):
    count = parts.shape[0]
    groups = [
        [4 * z + 2 * x + (kind ^ (z // (count // 2))) for z in range(count)]
        for x in range(2)
        for kind in range(2)
    ]
    return lax.all_to_all(parts, BLK + ("tensor",), 0, 0, axis_index_groups=groups, tiled=True)


def body(
    hidden, cotangent, token_loss_mask, adapter_down_factor, adapter_up_factor, sign_table_salts
):
    ex_rows, seq, width_half = hidden.shape
    blocks = lax.axis_size("z") * lax.axis_size("x")
    fast = 2 * blocks * ex_rows == LANES and ex_rows == 8
    send, ranks, near, start, kept, mixer = far_rows(
        sign_table_salts,
        token_loss_mask,
        adapter_down_factor,
        adapter_up_factor.T,
        hidden.reshape(ex_rows * seq, width_half),
        cotangent.reshape(ex_rows * seq, width_half),
        fast,
    )
    other = swap_cores(send)
    terms = (mixer, ranks, near_rows(start, kept, near), other)
    if fast:
        features, copies = feature_rows(*terms, ex_rows, blocks // 2)
        keep, send = pair_rows(features, swap_x(features), trade_z(copies), ex_rows)
        keep, send = join_halves(keep, swap_across(send))
        return sum_rows(keep, swap_cores(send))
    whole, _ = feature_rows(*terms, ex_rows, 1)
    share = ADAPTER_RANK * PROJ_ROWS // blocks
    parts = whole.reshape(ADAPTER_RANK, ex_rows, PROJ_ROWS // share, share)
    parts = parts.swapaxes(1, 2).reshape(blocks, ex_rows, share)
    features = lax.all_to_all(parts, BLK, 0, 0, tiled=True).reshape(blocks * ex_rows, share)
    pairs = jnp.einsum("ep,fp->ef", features, features, preferred_element_type=F32)
    pairs = pairs.reshape(blocks, ex_rows, blocks * ex_rows)
    total = jnp.sum(lax.all_to_all(pairs, BLK, 0, 0, tiled=True), axis=0)
    halves = total.reshape(2, ex_rows // 2, blocks * ex_rows)
    core = lax.axis_index("tensor")
    send = lax.dynamic_index_in_dim(halves, 1 - core, 0, keepdims=False)
    return lax.dynamic_index_in_dim(halves, core, 0, keepdims=False) + swap_cores(send)


def solution(mesh):
    groups, blocks, cores = (mesh.shape[name] for name in ("groups", "blk", "tensor"))
    devices = mesh.devices.reshape(groups, blocks // 2, 2, cores)
    placed = (
        P(("groups", "z", "x"), None, "tensor"),
        P(("groups", "z", "x"), None, "tensor"),
        P(("groups", "z", "x"), None),
        P(None, "tensor"),
        P("tensor", None),
        P(),
    )
    return jax.shard_map(
        body,
        mesh=Mesh(devices, ("groups", "z", "x", "tensor")),
        in_specs=placed,
        out_specs=P(("groups", "z", "x", "tensor"), None),
        check_vma=False,
    )
```

profile of v0, /device:TPU:0, one launch (start us, length us, event | category | flops | bytes accessed | tf_op | source)
XLA Modules:
  0.0 26.4 jit_solution(2522564859185529377)
XLA Ops:
  0.0 3.1 %shard_map.64 = (bf16[304,512]{1,0:T(8,128)(2,1)S(1)}, bf16[48,512]{1,0:T(8,128)(2,1)S(1)}, bf16[512,2048]{1,0:T(8,128)(2,1)S(1)}, s32[16,256]{1,0:T(8,128)S(1)}...) custom-call(s32[4]{0:T(128)} %salts_hbm.1, s32[8,64]{1,0:T(8,128)} %mask_hbm.1, bf16[16,2048]{1,0:T(8,128)(2,1)} %down_hbm.1, ...), custom_call_target="tpu_custom_call" | custom-call | tf_op jit(solution)/shard_map/pallas_call | solution.py:169
  3.1 0.5 %collective-permute-start = (bf16[304,512]{1,0:T(8,128)(2,1)S(1)}, bf16[304,512]{1,0:T(8,128)(2,1)S(1)}, u32[]{:S(2)}, u32[]{:S(2)}) collective-permute-start(bf16[304,512]{1,0:T(8,128)(2,1)S(1)} %get-tuple-element.22), channel_id=1, source_target_pairs={{0,1},{1,0},{2,3},{3,2},{4,5},{5,4},{6,7},{7,6},{8,9},{9,8},{10,11... | collective-permute-start | bytes 933896 | tf_op jit(solution)/shard_map/ppermute | solution.py:316
  3.7 1.0 %shard_map.65.own_ref = bf16[256,512]{1,0:T(8,128)(2,1)S(1)} custom-call(s32[16,256]{1,0:T(8,128)S(1)} %get-tuple-element.19.start_ref, f32[8,512]{1,0:T(8,128)S(1)} %get-tuple-element.20.kept_ref, bf16[512,2048]{1,0:T(8,128)(2,1)S(1)} %get-tuple-element.21.near_ref), custom_call_target="tpu_custom_call" | custom-call | flops 536870912 | bytes 2097152 | tf_op jit(solution)/shard_map/pallas_call | solution.py:208
  4.7 0.2 collective-permute-done.other_ref
  4.9 1.1 %shard_map.66 = (bf16[128,256]{1,0:T(8,128)(2,1)S(1)}, bf16[4,128,256]{2,1,0:T(8,128)(2,1)}) custom-call(bf16[128,96]{1,0:T(8,128)(2,1)S(1)} %get-tuple-element.17.mixer_ref, bf16[48,512]{1,0:T(8,128)(2,1)S(1)} %get-tuple-element.18.ranks_ref, bf16[256,512]{1,0:T(8,128)(2,1)S(1)} %shard_map.65.own_ref, bf16[304,512]{1,0:T(8,128)(2,1)S(1)} %collective-permute-done.other_ref), custom_call_target="tpu_custom_call" | custom-call | tf_op jit(solution)/shard_map/pallas_call | solution.py:237
  6.0 6.0 %all-to-all-start = ((bf16[4,128,256]{2,1,0:T(8,128)(2,1)}), bf16[4,128,256]{2,1,0:T(8,128)(2,1)S(1)}, u32[]{:S(2)}, u32[]{:S(2)}) async-start(bf16[4,128,256]{2,1,0:T(8,128)(2,1)} %get-tuple-element.24), calls=%async_computation | async-start | bytes 524288 | tf_op jit(solution)/shard_map/all_to_all | solution.py:334
  12.0 1.5 %collective-permute-start.1 = (bf16[128,256]{1,0:T(8,128)(2,1)S(1)}, bf16[128,256]{1,0:T(8,128)(2,1)S(1)}, u32[]{:S(2)}, u32[]{:S(2)}) collective-permute-start(bf16[128,256]{1,0:T(8,128)(2,1)S(1)} %get-tuple-element.23.own_ref), channel_id=1, source_target_pairs={{0,2},{2,0},{1,3},{3,1},{4,6},{6,4},{5,7},{7,5},{8,10},{10,8},{9,1... | collective-permute-start | bytes 196616 | tf_op jit(solution)/shard_map/ppermute | solution.py:324
  13.5 2.9 %collective-permute-done.1.near_ref = bf16[128,256]{1,0:T(8,128)(2,1)S(1)} collective-permute-done((bf16[128,256]{1,0:T(8,128)(2,1)S(1)}, bf16[128,256]{1,0:T(8,128)(2,1)S(1)}, u32[]{:S(2)}, u32[]{:S(2)}) %collective-permute-start.1) | collective-permute-done | bytes 65568 | tf_op jit(solution)/shard_map/ppermute | solution.py:324
  16.3 4.0 %all-to-all-done.got_ref = bf16[4,128,256]{2,1,0:T(8,128)(2,1)S(1)} async-done(((bf16[4,128,256]{2,1,0:T(8,128)(2,1)}), bf16[4,128,256]{2,1,0:T(8,128)(2,1)S(1)}, u32[]{:S(2)}, u32[]{:S(2)}) %all-to-all-start) | async-done | bytes 262176 | tf_op jit(solution)/shard_map/all_to_all | solution.py:334
  20.3 0.3 %shard_map.67 = (f32[8,128]{1,0:T(8,128)S(1)}, f32[8,128]{1,0:T(8,128)S(1)}) custom-call(bf16[128,256]{1,0:T(8,128)(2,1)S(1)} %get-tuple-element.23.own_ref, bf16[128,256]{1,0:T(8,128)(2,1)S(1)} %collective-permute-done.1.near_ref, bf16[4,128,256]{2,1,0:T(8,128)(2,1)S(1)} %all-to-all-done.got_ref), custom_call_target="tpu_custom_call" | custom-call | tf_op jit(solution)/shard_map/pallas_call | solution.py:269
  20.6 2.3 %collective-permute-start.2 = (f32[8,128]{1,0:T(8,128)S(1)}, f32[8,128]{1,0:T(8,128)S(1)}, u32[]{:S(2)}, u32[]{:S(2)}) collective-permute-start(f32[8,128]{1,0:T(8,128)S(1)} %get-tuple-element.26), channel_id=1, source_target_pairs={{0,3},{1,2},{2,1},{3,0},{4,7},{5,6},{6,5},{7,4},{8,11},{9,10},{10,... | collective-permute-start | bytes 12296 | tf_op jit(solution)/shard_map/ppermute | solution.py:320
  22.9 1.3 %collective-permute-done.2.got_ref = f32[8,128]{1,0:T(8,128)S(1)} collective-permute-done((f32[8,128]{1,0:T(8,128)S(1)}, f32[8,128]{1,0:T(8,128)S(1)}, u32[]{:S(2)}, u32[]{:S(2)}) %collective-permute-start.2) | collective-permute-done | bytes 4128 | tf_op jit(solution)/shard_map/ppermute | solution.py:320
  24.3 0.1 shard_map.68
  24.4 0.6 %collective-permute-start.3 = (f32[4,128]{1,0:T(4,128)S(1)}, f32[4,128]{1,0:T(4,128)S(1)}, u32[]{:S(2)}, u32[]{:S(2)}) collective-permute-start(f32[4,128]{1,0:T(4,128)S(1)} %get-tuple-element.28), channel_id=1, source_target_pairs={{0,1},{1,0},{2,3},{3,2},{4,5},{5,4},{6,7},{7,6},{8,9},{9,8},{10,11... | collective-permute-start | bytes 6152 | tf_op jit(solution)/shard_map/ppermute | solution.py:316
  25.0 0.8 %collective-permute-done.3.got_ref = f32[4,128]{1,0:T(4,128)S(1)} collective-permute-done((f32[4,128]{1,0:T(4,128)S(1)}, f32[4,128]{1,0:T(4,128)S(1)}, u32[]{:S(2)}, u32[]{:S(2)}) %collective-permute-start.3) | collective-permute-done | bytes 2080 | tf_op jit(solution)/shard_map/ppermute | solution.py:316
  25.8 0.6 %shard_map.69 = f32[4,64]{1,0:T(4,128)} custom-call(f32[4,128]{1,0:T(4,128)S(1)} %get-tuple-element.27.keep_ref, f32[4,128]{1,0:T(4,128)S(1)} %collective-permute-done.3.got_ref), custom_call_target="tpu_custom_call" | custom-call | tf_op jit(solution)/shard_map/pallas_call | solution.py:306
Async XLA Ops:
  3.1 1.8 %collective-permute-start = (bf16[304,512]{1,0:T(8,128)(2,1)S(1)}, bf16[304,512]{1,0:T(8,128)(2,1)S(1)}, u32[]{:S(2)}, u32[]{:S(2)}) collective-permute-start(bf16[304,512]{1,0:T(8,128)(2,1)S(1)} %get-tuple-element.22), channel_id=1, source_target_pairs={{0,1},{1,0},{2,3},{3,2},{4,5},{5,4},{6,7},{7,6},{8,9},{9,8},{10,11... | collective-permute-start | bytes 933896 | tf_op jit(solution)/shard_map/ppermute | solution.py:316
  6.0 14.3 %all-to-all-start = ((bf16[4,128,256]{2,1,0:T(8,128)(2,1)}), bf16[4,128,256]{2,1,0:T(8,128)(2,1)S(1)}, u32[]{:S(2)}, u32[]{:S(2)}) async-start(bf16[4,128,256]{2,1,0:T(8,128)(2,1)} %get-tuple-element.24), calls=%async_computation | async-start | bytes 524288 | tf_op jit(solution)/shard_map/all_to_all | solution.py:334
  12.0 4.4 %collective-permute-start.1 = (bf16[128,256]{1,0:T(8,128)(2,1)S(1)}, bf16[128,256]{1,0:T(8,128)(2,1)S(1)}, u32[]{:S(2)}, u32[]{:S(2)}) collective-permute-start(bf16[128,256]{1,0:T(8,128)(2,1)S(1)} %get-tuple-element.23.own_ref), channel_id=1, source_target_pairs={{0,2},{2,0},{1,3},{3,1},{4,6},{6,4},{5,7},{7,5},{8,10},{10,8},{9,1... | collective-permute-start | bytes 196616 | tf_op jit(solution)/shard_map/ppermute | solution.py:324
  20.6 3.7 %collective-permute-start.2 = (f32[8,128]{1,0:T(8,128)S(1)}, f32[8,128]{1,0:T(8,128)S(1)}, u32[]{:S(2)}, u32[]{:S(2)}) collective-permute-start(f32[8,128]{1,0:T(8,128)S(1)} %get-tuple-element.26), channel_id=1, source_target_pairs={{0,3},{1,2},{2,1},{3,0},{4,7},{5,6},{6,5},{7,4},{8,11},{9,10},{10,... | collective-permute-start | bytes 12296 | tf_op jit(solution)/shard_map/ppermute | solution.py:320
  24.4 1.4 %collective-permute-start.3 = (f32[4,128]{1,0:T(4,128)S(1)}, f32[4,128]{1,0:T(4,128)S(1)}, u32[]{:S(2)}, u32[]{:S(2)}) collective-permute-start(f32[4,128]{1,0:T(4,128)S(1)} %get-tuple-element.28), channel_id=1, source_target_pairs={{0,1},{1,0},{2,3},{3,2},{4,5},{5,4},{6,7},{7,6},{8,9},{9,8},{10,11... | collective-permute-start | bytes 6152 | tf_op jit(solution)/shard_map/ppermute | solution.py:316
where the time goes:
time: 26.6 us; the launch traced here: 26.4 us
  starting transfers between devices  10.9 us (41%)
  waiting for transfers between devices  9.19 us (35%)
  Pallas kernels  6.21 us (23%)
    all_to_all x1, starting transfers between devices, trade_z(): lax.all_to_all(parts, BLK + ('tensor',), 0, 0, axis_index_groups=groups,...  5.97 us
    all_to_all x1, waiting for transfers between devices, trade_z(): lax.all_to_all(parts, BLK + ('tensor',), 0, 0, axis_index_groups=groups,...  3.95 us
    pallas_call x1, Pallas kernels, far_rows(): pl.pallas_call(functools.partial(far_kernel, cross, ex_rows), out_shape=[...  3.14 us
    ppermute x1, waiting for transfers between devices, swap_x(): return lax.ppermute(value, 'x', [(0, 1), (1, 0)])  2.87 us
    ppermute x1, starting transfers between devices, swap_across(): return lax.ppermute(value, ('x', 'tensor'), [(i, i ^ 3) for i in range(4)])  2.34 us
    ppermute x1, starting transfers between devices, swap_x(): return lax.ppermute(value, 'x', [(0, 1), (1, 0)])  1.5 us
    ppermute x1, waiting for transfers between devices, swap_across(): return lax.ppermute(value, ('x', 'tensor'), [(i, i ^ 3) for i in range(4)])  1.33 us
    ppermute x2, starting transfers between devices, swap_cores(): return lax.ppermute(value, 'tensor', [(0, 1), (1, 0)])  1.14 us
  transfers between devices with their start and end apart: 5, of which 5 were waited for; matrix products, arithmetic and copies ran while one was open for 0% of the time, Pallas kernels for 4%

commit v1 on v0

--- a/solution.py
+++ b/solution.py
@@ -217,7 +217,7 @@
     )(start, kept, near)
 
 
-def feature_kernel(ex_rows, mixer_ref, ranks_ref, own_ref, other_ref, out_ref, copies_ref):
+def feature_kernel(ex_rows, mixer_ref, ranks_ref, own_ref, other_ref, out_ref):
     tokens = own_ref.shape[1]
     rows = ADAPTER_RANK * ex_rows
     pieces = jnp.concatenate([ranks_ref[...], other_ref[PROJ_ROWS:]], axis=0)
@@ -226,22 +226,15 @@
     coeffs = jnp.where(owned, coeffs, 0.0).astype(BF16)
     projected = lax.dot_general(coeffs, own_ref[...], NT, preferred_element_type=F32)
     projected += lax.dot_general(coeffs, other_ref[:PROJ_ROWS], NT, preferred_element_type=F32)
-    features = (projected * SCALE).astype(BF16)
-    out_ref[...] = features
-    for copy in range(copies_ref.shape[0]):
-        copies_ref[copy] = features
-
-
-def feature_rows(mixer, ranks, own, other, ex_rows, copies):
-    rows = ADAPTER_RANK * ex_rows
+    out_ref[...] = (projected * SCALE).astype(BF16)
+
+
+def feature_rows(mixer, ranks, own, other, ex_rows):
     return pl.pallas_call(
         functools.partial(feature_kernel, ex_rows),
-        out_shape=[
-            jax.ShapeDtypeStruct((rows, PROJ_ROWS), BF16),
-            jax.ShapeDtypeStruct((copies, rows, PROJ_ROWS), BF16),
-        ],
+        out_shape=jax.ShapeDtypeStruct((ADAPTER_RANK * ex_rows, PROJ_ROWS), BF16),
         in_specs=[VMEM] * 4,
-        out_specs=[VMEM] * 2,
+        out_specs=VMEM,
         compiler_params=SMALL,
     )(mixer, ranks, own, other)
 
@@ -252,27 +245,36 @@
     return jnp.where(iota(folded.shape, 1) % (2 * half) < half, folded, 0.0)
 
 
-def pair_kernel(ex_rows, own_ref, near_ref, got_ref, keep_ref, send_ref):
-    blocks, rows, _ = got_ref.shape
+def order_blocks(rows, wide):
+    z = lax.axis_index("z")
+    rows = jnp.where((z & 2) != 0, pltpu.roll(rows, 2 * wide, 1), rows)
+    even = (iota(rows.shape, 1) // wide) % 2 == 0
+    swapped = jnp.where(even, pltpu.roll(rows, LANES - wide, 1), pltpu.roll(rows, wide, 1))
+    return jnp.where((z & 1) != 0, swapped, rows)
+
+
+def pair_kernel(ex_rows, near_ref, *refs):
+    *z_refs, keep_ref, send_ref = refs
+    wide = 2 * ex_rows
     total = None
-    for row in range(0, rows, 2 * ex_rows):
-        part = slice(row, row + 2 * ex_rows)
-        left = jnp.concatenate([own_ref[part, :], near_ref[part, :]], axis=0)
-        right = jnp.concatenate([got_ref[b, part, :] for b in range(blocks)] * 2, axis=0)
+    for row in range(0, near_ref.shape[0], wide):
+        part = slice(row, row + wide)
+        left = jnp.concatenate([z_refs[0][part, :], near_ref[part, :]], axis=0)
+        right = jnp.concatenate([ref[part, :] for ref in z_refs] * 2, axis=0)
         term = lax.dot_general(left, right, NT, preferred_element_type=F32)
         total = term if total is None else total + term
-    keep_ref[...] = fold_ranks(total[: 2 * ex_rows])
-    send_ref[...] = fold_ranks(total[2 * ex_rows :])
-
-
-def pair_rows(own, near, got, ex_rows):
+    keep_ref[...] = order_blocks(fold_ranks(total[:wide]), wide)
+    send_ref[...] = order_blocks(fold_ranks(total[wide:]), wide)
+
+
+def pair_rows(near, by_z, ex_rows):
     return pl.pallas_call(
         functools.partial(pair_kernel, ex_rows),
         out_shape=[jax.ShapeDtypeStruct((ex_rows, LANES), F32)] * 2,
-        in_specs=[VMEM] * 3,
+        in_specs=[VMEM] * (1 + len(by_z)),
         out_specs=[VMEM] * 2,
         compiler_params=SMALL,
-    )(own, near, got)
+    )(near, *by_z)
 
 
 def halves_kernel(own_ref, got_ref, keep_ref, send_ref):
@@ -324,14 +326,9 @@
     return lax.ppermute(value, "x", [(0, 1), (1, 0)])
 
 
-def trade_z(parts):
-    count = parts.shape[0]
-    groups = [
-        [4 * z + 2 * x + (kind ^ (z // (count // 2))) for z in range(count)]
-        for x in range(2)
-        for kind in range(2)
-    ]
-    return lax.all_to_all(parts, BLK + ("tensor",), 0, 0, axis_index_groups=groups, tiled=True)
+def swap_z(value, step):
+    other = 4 * step + (step > 1)
+    return lax.ppermute(value, BLK + ("tensor",), [(i, i ^ other) for i in range(16)])
 
 
 def body(
@@ -339,7 +336,7 @@
 ):
     ex_rows, seq, width_half = hidden.shape
     blocks = lax.axis_size("z") * lax.axis_size("x")
-    fast = 2 * blocks * ex_rows == LANES and ex_rows == 8
+    fast = blocks == 8 and ex_rows == 8
     send, ranks, near, start, kept, mixer = far_rows(
         sign_table_salts,
         token_loss_mask,
@@ -351,14 +348,17 @@
     )
     other = swap_cores(send)
     terms = (mixer, ranks, near_rows(start, kept, near), other)
+    features = feature_rows(*terms, ex_rows)
     if fast:
-        features, copies = feature_rows(*terms, ex_rows, blocks // 2)
-        keep, send = pair_rows(features, swap_x(features), trade_z(copies), ex_rows)
+        third = swap_z(features, 3)
+        second = swap_z(features, 2)
+        first = swap_z(features, 1)
+        near = swap_x(features)
+        keep, send = pair_rows(near, (features, first, second, third), ex_rows)
         keep, send = join_halves(keep, swap_across(send))
         return sum_rows(keep, swap_cores(send))
-    whole, _ = feature_rows(*terms, ex_rows, 1)
     share = ADAPTER_RANK * PROJ_ROWS // blocks
-    parts = whole.reshape(ADAPTER_RANK, ex_rows, PROJ_ROWS // share, share)
+    parts = features.reshape(ADAPTER_RANK, ex_rows, PROJ_ROWS // share, share)
     parts = parts.swapaxes(1, 2).reshape(blocks, ex_rows, share)
     features = lax.all_to_all(parts, BLK, 0, 0, tiled=True).reshape(blocks * ex_rows, share)
     pairs = jnp.einsum("ep,fp->ef", features, features, preferred_element_type=F32)

time: 26.6 us -> 21.5 us (0.81)
  waiting for transfers between devices: 9.19 us -> 6.71 us
  starting transfers between devices: 10.9 us -> 8.96 us
  Pallas kernels: 6.21 us -> 5.64 us
    all_to_all x1 -> x0, starting transfers between devices: 5.97 us -> none  [trade_z(): lax.all_to_all(parts, BLK + ('tensor',), 0, 0, axis_index_groups=groups,...]
    ppermute x0 -> x3, starting transfers between devices: none -> 5.43 us  [swap_z(): lax.ppermute(value, BLK + ('tensor',), [(i, i ^ other) for i in range(16)])]
    all_to_all x1 -> x0, waiting for transfers between devices: 3.95 us -> none  [trade_z(): lax.all_to_all(parts, BLK + ('tensor',), 0, 0, axis_index_groups=groups,...]
    ppermute x0 -> x3, waiting for transfers between devices: none -> 3.69 us  [swap_z(): lax.ppermute(value, BLK + ('tensor',), [(i, i ^ other) for i in range(16)])]
    ppermute x1, waiting for transfers between devices: 2.87 us -> 0.01 us  [swap_x(): return lax.ppermute(value, 'x', [(0, 1), (1, 0)])]
    ppermute x1, starting transfers between devices: 2.34 us -> 1.27 us  [swap_across(): return lax.ppermute(value, ('x', 'tensor'), [(i, i ^ 3) for i in range(4)])]
    pallas_call x1, Pallas kernels: 1.08 us -> 0.37 us  [feature_rows(): pl.pallas_call(functools.partial(feature_kernel, ex_rows), out_shape=jax....]
    ppermute x2, starting transfers between devices: 1.14 us -> 0.67 us  [swap_cores(): return lax.ppermute(value, 'tensor', [(0, 1), (1, 0)])]
  transfers between devices with their start and end apart: 5 -> 7, of which waited for: 5 -> 5; matrix products, arithmetic and copies ran while one was open for 0% -> 0% of each run, Pallas kernels for 4% -> 5%
where the time goes in v1:
time: 21.5 us; the launch traced here: 21.3 us
  starting transfers between devices  8.96 us (42%)
  waiting for transfers between devices  6.71 us (31%)
  Pallas kernels  5.64 us (26%)
    ppermute x3, starting transfers between devices, swap_z(): lax.ppermute(value, BLK + ('tensor',), [(i, i ^ other) for i in range(16)])  5.43 us
    ppermute x3, waiting for transfers between devices, swap_z(): lax.ppermute(value, BLK + ('tensor',), [(i, i ^ other) for i in range(16)])  3.69 us
    pallas_call x1, Pallas kernels, far_rows(): pl.pallas_call(functools.partial(far_kernel, cross, ex_rows), out_shape=[...  3.14 us
    ppermute x1, waiting for transfers between devices, swap_across(): return lax.ppermute(value, ('x', 'tensor'), [(i, i ^ 3) for i in range(4)])  1.79 us
    ppermute x1, starting transfers between devices, swap_x(): return lax.ppermute(value, 'x', [(0, 1), (1, 0)])  1.6 us
    ppermute x1, starting transfers between devices, swap_across(): return lax.ppermute(value, ('x', 'tensor'), [(i, i ^ 3) for i in range(4)])  1.27 us
    ppermute x2, waiting for transfers between devices, swap_cores(): return lax.ppermute(value, 'tensor', [(0, 1), (1, 0)])  1.22 us
    pallas_call x1, Pallas kernels, near_rows(): pl.pallas_call(near_kernel, out_shape=jax.ShapeDtypeStruct((PROJ_ROWS, to...  1.02 us
  transfers between devices with their start and end apart: 7, of which 5 were waited for; matrix products, arithmetic and copies ran while one was open for 0% of the time, Pallas kernels for 5%

profile of v1, /device:TPU:0, one launch (start us, length us, event | category | flops | bytes accessed | tf_op | source)
XLA Modules:
  0.0 21.3 jit_solution(6387574229321934548)
XLA Ops:
  0.0 3.1 %shard_map.64 = (bf16[304,512]{1,0:T(8,128)(2,1)S(1)}, bf16[48,512]{1,0:T(8,128)(2,1)S(1)}, bf16[512,2048]{1,0:T(8,128)(2,1)S(1)}, s32[16,256]{1,0:T(8,128)S(1)}...) custom-call(s32[4]{0:T(128)} %salts_hbm.1, s32[8,64]{1,0:T(8,128)} %mask_hbm.1, bf16[16,2048]{1,0:T(8,128)(2,1)} %down_hbm.1, ...), custom_call_target="tpu_custom_call" | custom-call | tf_op jit(solution)/shard_map/pallas_call | solution.py:169
  3.1 0.5 %collective-permute-start = (bf16[304,512]{1,0:T(8,128)(2,1)S(1)}, bf16[304,512]{1,0:T(8,128)(2,1)S(1)}, u32[]{:S(2)}, u32[]{:S(2)}) collective-permute-start(bf16[304,512]{1,0:T(8,128)(2,1)S(1)} %get-tuple-element.20), channel_id=1, source_target_pairs={{0,1},{1,0},{2,3},{3,2},{4,5},{5,4},{6,7},{7,6},{8,9},{9,8},{10,11... | collective-permute-start | bytes 933896 | tf_op jit(solution)/shard_map/ppermute | solution.py:318
  3.7 1.0 %shard_map.65.own_ref = bf16[256,512]{1,0:T(8,128)(2,1)S(1)} custom-call(s32[16,256]{1,0:T(8,128)S(1)} %get-tuple-element.17.start_ref, f32[8,512]{1,0:T(8,128)S(1)} %get-tuple-element.18.kept_ref, bf16[512,2048]{1,0:T(8,128)(2,1)S(1)} %get-tuple-element.19.near_ref), custom_call_target="tpu_custom_call" | custom-call | flops 536870912 | bytes 2097152 | tf_op jit(solution)/shard_map/pallas_call | solution.py:208
  4.7 0.2 collective-permute-done.other_ref
  4.9 0.4 %shard_map.66.refs_0_ = bf16[128,256]{1,0:T(8,128)(2,1)S(1)} custom-call(bf16[128,96]{1,0:T(8,128)(2,1)S(1)} %get-tuple-element.15.mixer_ref, bf16[48,512]{1,0:T(8,128)(2,1)S(1)} %get-tuple-element.16.ranks_ref, bf16[256,512]{1,0:T(8,128)(2,1)S(1)} %shard_map.65.own_ref, bf16[304,512]{1,0:T(8,128)(2,1)S(1)} %collective-permute-done.other_ref), custom_call_target="tpu_custom_call" | custom-call | tf_op jit(solution)/shard_map/pallas_call | solution.py:233
  5.3 4.8 %collective-permute-start.4 = (bf16[128,256]{1,0:T(8,128)(2,1)S(1)}, bf16[128,256]{1,0:T(8,128)(2,1)S(1)}, u32[]{:S(2)}, u32[]{:S(2)}) collective-permute-start(bf16[128,256]{1,0:T(8,128)(2,1)S(1)} %shard_map.66.refs_0_), channel_id=1, source_target_pairs={{0,13},{1,12},{2,15},{3,14},{4,9},{5,8},{6,11},{7,10},{8,5},{9,4},... | collective-permute-start | bytes 196616 | tf_op jit(solution)/shard_map/ppermute | solution.py:331
  10.1 0.0 collective-permute-start.3
  10.1 0.7 %collective-permute-start.2 = (bf16[128,256]{1,0:T(8,128)(2,1)S(1)}, bf16[128,256]{1,0:T(8,128)(2,1)S(1)}, u32[]{:S(2)}, u32[]{:S(2)}) collective-permute-start(bf16[128,256]{1,0:T(8,128)(2,1)S(1)} %shard_map.66.refs_0_), channel_id=1, source_target_pairs={{0,4},{1,5},{2,6},{3,7},{4,0},{5,1},{6,2},{7,3},{8,12},{9,13},{10,... | collective-permute-start | bytes 196616 | tf_op jit(solution)/shard_map/ppermute | solution.py:331
  10.7 1.6 %collective-permute-start.1 = (bf16[128,256]{1,0:T(8,128)(2,1)S(1)}, bf16[128,256]{1,0:T(8,128)(2,1)S(1)}, u32[]{:S(2)}, u32[]{:S(2)}) collective-permute-start(bf16[128,256]{1,0:T(8,128)(2,1)S(1)} %shard_map.66.refs_0_), channel_id=1, source_target_pairs={{0,2},{2,0},{1,3},{3,1},{4,6},{6,4},{5,7},{7,5},{8,10},{10,8},{9,1... | collective-permute-start | bytes 196616 | tf_op jit(solution)/shard_map/ppermute | solution.py:326
  12.3 0.3 %collective-permute-done.4.refs_3_ = bf16[128,256]{1,0:T(8,128)(2,1)S(1)} collective-permute-done((bf16[128,256]{1,0:T(8,128)(2,1)S(1)}, bf16[128,256]{1,0:T(8,128)(2,1)S(1)}, u32[]{:S(2)}, u32[]{:S(2)}) %collective-permute-start.4) | collective-permute-done | bytes 65568 | tf_op jit(solution)/shard_map/ppermute | solution.py:331
  12.6 3.4 %collective-permute-done.3.refs_2_ = bf16[128,256]{1,0:T(8,128)(2,1)S(1)} collective-permute-done((bf16[128,256]{1,0:T(8,128)(2,1)S(1)}, bf16[128,256]{1,0:T(8,128)(2,1)S(1)}, u32[]{:S(2)}, u32[]{:S(2)}) %collective-permute-start.3) | collective-permute-done | bytes 65568 | tf_op jit(solution)/shard_map/ppermute | solution.py:331
  16.0 0.0 collective-permute-done.2.refs_1_
  16.0 0.0 collective-permute-done.1.near_ref
  16.0 0.5 %shard_map.67 = (f32[8,128]{1,0:T(8,128)S(1)}, f32[8,128]{1,0:T(8,128)S(1)}) custom-call(bf16[128,256]{1,0:T(8,128)(2,1)S(1)} %collective-permute-done.1.near_ref, bf16[128,256]{1,0:T(8,128)(2,1)S(1)} %shard_map.66.refs_0_, bf16[128,256]{1,0:T(8,128)(2,1)S(1)} %collective-permute-done.2.refs_1_, bf16[128,256]{1,0:T(8,128)(2,1)S(1)} %collective-permute-done.3.refs_2_, ...), custom_call_target="tpu_custom_call" | custom-call | tf_op jit(solution)/shard_map/pallas_call | solution.py:271
  16.5 1.3 %collective-permute-start.5 = (f32[8,128]{1,0:T(8,128)S(1)}, f32[8,128]{1,0:T(8,128)S(1)}, u32[]{:S(2)}, u32[]{:S(2)}) collective-permute-start(f32[8,128]{1,0:T(8,128)S(1)} %get-tuple-element.22), channel_id=1, source_target_pairs={{0,3},{1,2},{2,1},{3,0},{4,7},{5,6},{6,5},{7,4},{8,11},{9,10},{10,... | collective-permute-start | bytes 12296 | tf_op jit(solution)/shard_map/ppermute | solution.py:322
  17.7 1.8 %collective-permute-done.5.got_ref = f32[8,128]{1,0:T(8,128)S(1)} collective-permute-done((f32[8,128]{1,0:T(8,128)S(1)}, f32[8,128]{1,0:T(8,128)S(1)}, u32[]{:S(2)}, u32[]{:S(2)}) %collective-permute-start.5) | collective-permute-done | bytes 4128 | tf_op jit(solution)/shard_map/ppermute | solution.py:322
  19.5 0.1 shard_map.68
  19.6 0.1 collective-permute-start.6
  19.7 1.0 %collective-permute-done.6.got_ref = f32[4,128]{1,0:T(4,128)S(1)} collective-permute-done((f32[4,128]{1,0:T(4,128)S(1)}, f32[4,128]{1,0:T(4,128)S(1)}, u32[]{:S(2)}, u32[]{:S(2)}) %collective-permute-start.6) | collective-permute-done | bytes 2080 | tf_op jit(solution)/shard_map/ppermute | solution.py:318
  20.8 0.6 %shard_map.69 = f32[4,64]{1,0:T(4,128)} custom-call(f32[4,128]{1,0:T(4,128)S(1)} %get-tuple-element.23.keep_ref, f32[4,128]{1,0:T(4,128)S(1)} %collective-permute-done.6.got_ref), custom_call_target="tpu_custom_call" | custom-call | tf_op jit(solution)/shard_map/pallas_call | solution.py:308
Async XLA Ops:
  3.1 1.8 %collective-permute-start = (bf16[304,512]{1,0:T(8,128)(2,1)S(1)}, bf16[304,512]{1,0:T(8,128)(2,1)S(1)}, u32[]{:S(2)}, u32[]{:S(2)}) collective-permute-start(bf16[304,512]{1,0:T(8,128)(2,1)S(1)} %get-tuple-element.20), channel_id=1, source_target_pairs={{0,1},{1,0},{2,3},{3,2},{4,5},{5,4},{6,7},{7,6},{8,9},{9,8},{10,11... | collective-permute-start | bytes 933896 | tf_op jit(solution)/shard_map/ppermute | solution.py:318
  5.3 7.3 %collective-permute-start.4 = (bf16[128,256]{1,0:T(8,128)(2,1)S(1)}, bf16[128,256]{1,0:T(8,128)(2,1)S(1)}, u32[]{:S(2)}, u32[]{:S(2)}) collective-permute-start(bf16[128,256]{1,0:T(8,128)(2,1)S(1)} %shard_map.66.refs_0_), channel_id=1, source_target_pairs={{0,13},{1,12},{2,15},{3,14},{4,9},{5,8},{6,11},{7,10},{8,5},{9,4},... | collective-permute-start | bytes 196616 | tf_op jit(solution)/shard_map/ppermute | solution.py:331
  10.1 5.9 %collective-permute-start.3 = (bf16[128,256]{1,0:T(8,128)(2,1)S(1)}, bf16[128,256]{1,0:T(8,128)(2,1)S(1)}, u32[]{:S(2)}, u32[]{:S(2)}) collective-permute-start(bf16[128,256]{1,0:T(8,128)(2,1)S(1)} %shard_map.66.refs_0_), channel_id=1, source_target_pairs={{0,9},{1,8},{2,11},{3,10},{4,13},{5,12},{6,15},{7,14},{8,1},{9,0},... | collective-permute-start | bytes 196616 | tf_op jit(solution)/shard_map/ppermute | solution.py:331
  10.1 5.9 %collective-permute-start.2 = (bf16[128,256]{1,0:T(8,128)(2,1)S(1)}, bf16[128,256]{1,0:T(8,128)(2,1)S(1)}, u32[]{:S(2)}, u32[]{:S(2)}) collective-permute-start(bf16[128,256]{1,0:T(8,128)(2,1)S(1)} %shard_map.66.refs_0_), channel_id=1, source_target_pairs={{0,4},{1,5},{2,6},{3,7},{4,0},{5,1},{6,2},{7,3},{8,12},{9,13},{10,... | collective-permute-start | bytes 196616 | tf_op jit(solution)/shard_map/ppermute | solution.py:331
  10.7 5.3 %collective-permute-start.1 = (bf16[128,256]{1,0:T(8,128)(2,1)S(1)}, bf16[128,256]{1,0:T(8,128)(2,1)S(1)}, u32[]{:S(2)}, u32[]{:S(2)}) collective-permute-start(bf16[128,256]{1,0:T(8,128)(2,1)S(1)} %shard_map.66.refs_0_), channel_id=1, source_target_pairs={{0,2},{2,0},{1,3},{3,1},{4,6},{6,4},{5,7},{7,5},{8,10},{10,8},{9,1... | collective-permute-start | bytes 196616 | tf_op jit(solution)/shard_map/ppermute | solution.py:326
  16.5 3.1 %collective-permute-start.5 = (f32[8,128]{1,0:T(8,128)S(1)}, f32[8,128]{1,0:T(8,128)S(1)}, u32[]{:S(2)}, u32[]{:S(2)}) collective-permute-start(f32[8,128]{1,0:T(8,128)S(1)} %get-tuple-element.22), channel_id=1, source_target_pairs={{0,3},{1,2},{2,1},{3,0},{4,7},{5,6},{6,5},{7,4},{8,11},{9,10},{10,... | collective-permute-start | bytes 12296 | tf_op jit(solution)/shard_map/ppermute | solution.py:322
  19.6 1.2 %collective-permute-start.6 = (f32[4,128]{1,0:T(4,128)S(1)}, f32[4,128]{1,0:T(4,128)S(1)}, u32[]{:S(2)}, u32[]{:S(2)}) collective-permute-start(f32[4,128]{1,0:T(4,128)S(1)} %get-tuple-element.24), channel_id=1, source_target_pairs={{0,1},{1,0},{2,3},{3,2},{4,5},{5,4},{6,7},{7,6},{8,9},{9,8},{10,11... | collective-permute-start | bytes 6152 | tf_op jit(solution)/shard_map/ppermute | solution.py:318

commit v2 on v1

--- a/solution.py
+++ b/solution.py
@@ -253,51 +253,71 @@
     return jnp.where((z & 1) != 0, swapped, rows)
 
 
-def pair_kernel(ex_rows, near_ref, *refs):
-    *z_refs, keep_ref, send_ref = refs
+def back_lanes(rows, ex_rows):
+    z = lax.axis_index("z")
+    lane = iota(rows.shape, 1)
+    both = rows + pltpu.roll(rows, LANES - ex_rows, 1)
+    both = jnp.where(lane % (4 * ex_rows) < 2 * ex_rows, both, 0.0)
+    both = jnp.where((z & 1) != 0, pltpu.roll(both, 2 * ex_rows, 1), both)
+    return jnp.where(lane // (2 * ex_rows) == z, both, 0.0)
+
+
+def pair_kernel(ex_rows, own_ref, near_ref, far_ref, first_ref, keep_ref, send_ref, back_ref):
     wide = 2 * ex_rows
-    total = None
-    for row in range(0, near_ref.shape[0], wide):
+    low_x = lax.axis_index("x") == 0
+    total = back = None
+    for row in range(0, own_ref.shape[0], wide):
         part = slice(row, row + wide)
-        left = jnp.concatenate([z_refs[0][part, :], near_ref[part, :]], axis=0)
-        right = jnp.concatenate([ref[part, :] for ref in z_refs] * 2, axis=0)
+        own, near, far, first = (
+            ref[part, :] for ref in (own_ref, near_ref, far_ref, first_ref)
+        )
+        left = jnp.concatenate([own, near], axis=0)
+        right = jnp.concatenate([own, first, far, far] * 2, axis=0)
         term = lax.dot_general(left, right, NT, preferred_element_type=F32)
         total = term if total is None else total + term
-    keep_ref[...] = order_blocks(fold_ranks(total[:wide]), wide)
-    send_ref[...] = order_blocks(fold_ranks(total[wide:]), wide)
-
-
-def pair_rows(near, by_z, ex_rows):
+        by_x = [jnp.where(low_x, own, near), jnp.where(low_x, near, own)]
+        right = jnp.concatenate(by_x * 4, axis=0)
+        term = lax.dot_general(far, right, NT, preferred_element_type=F32)
+        back = term if back is None else back + term
+    far_block = jnp.where(lax.axis_index("z") < 2, 2, 3)
+    block = iota((ex_rows, LANES), 1) // wide % 4
+    here = (block < 2) | (block == far_block)
+    for out_ref, rows in ((keep_ref, total[:wide]), (send_ref, total[wide:])):
+        out_ref[...] = order_blocks(jnp.where(here, fold_ranks(rows), 0.0), wide)
+    back_ref[...] = back_lanes(fold_ranks(back), ex_rows)
+
+
+def pair_rows(own, near, far, first, ex_rows):
     return pl.pallas_call(
         functools.partial(pair_kernel, ex_rows),
-        out_shape=[jax.ShapeDtypeStruct((ex_rows, LANES), F32)] * 2,
-        in_specs=[VMEM] * (1 + len(by_z)),
-        out_specs=[VMEM] * 2,
-        compiler_params=SMALL,
-    )(near, *by_z)
-
-
-def halves_kernel(own_ref, got_ref, keep_ref, send_ref):
+        out_shape=[jax.ShapeDtypeStruct((ex_rows, LANES), F32)] * 3,
+        in_specs=[VMEM] * 4,
+        out_specs=[VMEM] * 3,
+        compiler_params=SMALL,
+    )(own, near, far, first)
+
+
+def halves_kernel(own_ref, got_ref, back_ref, keep_ref, send_ref):
     ex_rows, _ = own_ref.shape
     low_x = lax.axis_index("x") == 0
     first = jnp.where(low_x, own_ref[...], got_ref[...])
     second = jnp.where(low_x, got_ref[...], own_ref[...])
-    total = first + pltpu.roll(second, ex_rows, 1)
+    total = first + pltpu.roll(second, ex_rows, 1) + back_ref[...]
     half = keep_ref.shape[0]
     low = lax.axis_index("tensor") == 0
     keep_ref[...] = jnp.where(low, total[:half], total[half:])
     send_ref[...] = jnp.where(low, total[half:], total[:half])
 
 
-def join_halves(own, got):
+def join_halves(own, got, back):
     rows, lanes = own.shape
     return pl.pallas_call(
         halves_kernel,
         out_shape=[jax.ShapeDtypeStruct((rows // 2, lanes), F32)] * 2,
-        in_specs=[VMEM] * 2,
+        in_specs=[VMEM] * 3,
         out_specs=[VMEM] * 2,
         compiler_params=SMALL,
-    )(own, got)
+    )(own, got, back)
 
 
 def sum_kernel(keep_ref, got_ref, out_ref):
@@ -326,9 +346,13 @@
     return lax.ppermute(value, "x", [(0, 1), (1, 0)])
 
 
-def swap_z(value, step):
-    other = 4 * step + (step > 1)
-    return lax.ppermute(value, BLK + ("tensor",), [(i, i ^ other) for i in range(16)])
+def send_z(value, targets):
+    pairs = []
+    for z, target in enumerate(targets):
+        for x in range(2):
+            for kind in range(2):
+                pairs.append(tuple(4 * at + 2 * x + (kind ^ (at // 2)) for at in (z, target)))
+    return lax.ppermute(value, BLK + ("tensor",), pairs)
 
 
 def body(
@@ -350,12 +374,12 @@
     terms = (mixer, ranks, near_rows(start, kept, near), other)
     features = feature_rows(*terms, ex_rows)
     if fast:
-        third = swap_z(features, 3)
-        second = swap_z(features, 2)
-        first = swap_z(features, 1)
+        first = send_z(features, (1, 0, 3, 2))
+        far = send_z(features, (3, 2, 0, 1))
         near = swap_x(features)
-        keep, send = pair_rows(near, (features, first, second, third), ex_rows)
-        keep, send = join_halves(keep, swap_across(send))
+        keep, send, back = pair_rows(features, near, far, first, ex_rows)
+        back = send_z(back, (2, 3, 1, 0))
+        keep, send = join_halves(keep, swap_across(send), back)
         return sum_rows(keep, swap_cores(send))
     share = ADAPTER_RANK * PROJ_ROWS // blocks
     parts = features.reshape(ADAPTER_RANK, ex_rows, PROJ_ROWS // share, share)

time: 21.5 us -> 23.6 us (1.098)
  starting transfers between devices: 8.96 us -> 10.4 us
  waiting for transfers between devices: 6.71 us -> 7.3 us
    ppermute x3, waiting for transfers between devices: 3.69 us -> 6.2 us  [send_z(): return lax.ppermute(value, BLK + ('tensor',), pairs)]
    ppermute x1, waiting for transfers between devices: 1.79 us -> 0.07 us  [swap_across(): return lax.ppermute(value, ('x', 'tensor'), [(i, i ^ 3) for i in range(4)])]
    ppermute x3, starting transfers between devices: 5.43 us -> 6.69 us  [send_z(): return lax.ppermute(value, BLK + ('tensor',), pairs)]
    ppermute x2, starting transfers between devices: 0.67 us -> 0.96 us  [swap_cores(): return lax.ppermute(value, 'tensor', [(0, 1), (1, 0)])]
  transfers between devices with their start and end apart: 7 -> 7, of which waited for: 5 -> 5; matrix products, arithmetic and copies ran while one was open for 0% -> 0% of each run, Pallas kernels for 5% -> 4%
where the time goes in v2:
time: 23.6 us; the launch traced here: 23.5 us
  starting transfers between devices  10.4 us (44%)
  waiting for transfers between devices  7.3 us (31%)
  Pallas kernels  5.77 us (24%)
    ppermute x3, starting transfers between devices, send_z(): return lax.ppermute(value, BLK + ('tensor',), pairs)  6.69 us
    ppermute x3, waiting for transfers between devices, send_z(): return lax.ppermute(value, BLK + ('tensor',), pairs)  6.2 us
    pallas_call x1, Pallas kernels, far_rows(): pl.pallas_call(functools.partial(far_kernel, cross, ex_rows), out_shape=[...  3.14 us
    ppermute x1, starting transfers between devices, swap_x(): return lax.ppermute(value, 'x', [(0, 1), (1, 0)])  1.49 us
    ppermute x1, starting transfers between devices, swap_across(): return lax.ppermute(value, ('x', 'tensor'), [(i, i ^ 3) for i in range(4)])  1.24 us
    ppermute x2, waiting for transfers between devices, swap_cores(): return lax.ppermute(value, 'tensor', [(0, 1), (1, 0)])  1.03 us
    pallas_call x1, Pallas kernels, near_rows(): pl.pallas_call(near_kernel, out_shape=jax.ShapeDtypeStruct((PROJ_ROWS, to...  1.02 us
    ppermute x2, starting transfers between devices, swap_cores(): return lax.ppermute(value, 'tensor', [(0, 1), (1, 0)])  0.96 us
  transfers between devices with their start and end apart: 7, of which 5 were waited for; matrix products, arithmetic and copies ran while one was open for 0% of the time, Pallas kernels for 4%

profile of v2, /device:TPU:0, one launch (start us, length us, event | category | flops | bytes accessed | tf_op | source)
XLA Modules:
  0.0 23.5 jit_solution(12843225612924884001)
XLA Ops:
  0.0 3.1 %shard_map.64 = (bf16[304,512]{1,0:T(8,128)(2,1)S(1)}, bf16[48,512]{1,0:T(8,128)(2,1)S(1)}, bf16[512,2048]{1,0:T(8,128)(2,1)S(1)}, s32[16,256]{1,0:T(8,128)S(1)}...) custom-call(s32[4]{0:T(128)} %salts_hbm.1, s32[8,64]{1,0:T(8,128)} %mask_hbm.1, bf16[16,2048]{1,0:T(8,128)(2,1)} %down_hbm.1, ...), custom_call_target="tpu_custom_call" | custom-call | tf_op jit(solution)/shard_map/pallas_call | solution.py:169
  3.1 0.5 %collective-permute-start = (bf16[304,512]{1,0:T(8,128)(2,1)S(1)}, bf16[304,512]{1,0:T(8,128)(2,1)S(1)}, u32[]{:S(2)}, u32[]{:S(2)}) collective-permute-start(bf16[304,512]{1,0:T(8,128)(2,1)S(1)} %get-tuple-element.21), channel_id=1, source_target_pairs={{0,1},{1,0},{2,3},{3,2},{4,5},{5,4},{6,7},{7,6},{8,9},{9,8},{10,11... | collective-permute-start | bytes 933896 | tf_op jit(solution)/shard_map/ppermute | solution.py:338
  3.7 1.0 %shard_map.65.own_ref = bf16[256,512]{1,0:T(8,128)(2,1)S(1)} custom-call(s32[16,256]{1,0:T(8,128)S(1)} %get-tuple-element.18.start_ref, f32[8,512]{1,0:T(8,128)S(1)} %get-tuple-element.19.kept_ref, bf16[512,2048]{1,0:T(8,128)(2,1)S(1)} %get-tuple-element.20.near_ref), custom_call_target="tpu_custom_call" | custom-call | flops 536870912 | bytes 2097152 | tf_op jit(solution)/shard_map/pallas_call | solution.py:208
  4.7 0.2 collective-permute-done.other_ref
  4.9 0.4 %shard_map.66.own_ref = bf16[128,256]{1,0:T(8,128)(2,1)S(1)} custom-call(bf16[128,96]{1,0:T(8,128)(2,1)S(1)} %get-tuple-element.16.mixer_ref, bf16[48,512]{1,0:T(8,128)(2,1)S(1)} %get-tuple-element.17.ranks_ref, bf16[256,512]{1,0:T(8,128)(2,1)S(1)} %shard_map.65.own_ref, bf16[304,512]{1,0:T(8,128)(2,1)S(1)} %collective-permute-done.other_ref), custom_call_target="tpu_custom_call" | custom-call | tf_op jit(solution)/shard_map/pallas_call | solution.py:233
  5.3 3.0 %collective-permute-start.3 = (bf16[128,256]{1,0:T(8,128)(2,1)S(1)}, bf16[128,256]{1,0:T(8,128)(2,1)S(1)}, u32[]{:S(2)}, u32[]{:S(2)}) collective-permute-start(bf16[128,256]{1,0:T(8,128)(2,1)S(1)} %shard_map.66.own_ref), channel_id=1, source_target_pairs={{0,4},{1,5},{2,6},{3,7},{4,0},{5,1},{6,2},{7,3},{9,13},{8,12},{11,... | collective-permute-start | bytes 196616 | tf_op jit(solution)/shard_map/ppermute | solution.py:355
  8.3 1.9 %collective-permute-start.2 = (bf16[128,256]{1,0:T(8,128)(2,1)S(1)}, bf16[128,256]{1,0:T(8,128)(2,1)S(1)}, u32[]{:S(2)}, u32[]{:S(2)}) collective-permute-start(bf16[128,256]{1,0:T(8,128)(2,1)S(1)} %shard_map.66.own_ref), channel_id=1, source_target_pairs={{0,13},{1,12},{2,15},{3,14},{4,9},{5,8},{6,11},{7,10},{9,0},{8,1},... | collective-permute-start | bytes 196616 | tf_op jit(solution)/shard_map/ppermute | solution.py:355
  10.2 1.5 %collective-permute-start.1 = (bf16[128,256]{1,0:T(8,128)(2,1)S(1)}, bf16[128,256]{1,0:T(8,128)(2,1)S(1)}, u32[]{:S(2)}, u32[]{:S(2)}) collective-permute-start(bf16[128,256]{1,0:T(8,128)(2,1)S(1)} %shard_map.66.own_ref), channel_id=1, source_target_pairs={{0,2},{2,0},{1,3},{3,1},{4,6},{6,4},{5,7},{7,5},{8,10},{10,8},{9,1... | collective-permute-start | bytes 196616 | tf_op jit(solution)/shard_map/ppermute | solution.py:346
  11.7 0.0 collective-permute-done.3.first_ref
  11.7 3.2 %collective-permute-done.2.far_ref = bf16[128,256]{1,0:T(8,128)(2,1)S(1)} collective-permute-done((bf16[128,256]{1,0:T(8,128)(2,1)S(1)}, bf16[128,256]{1,0:T(8,128)(2,1)S(1)}, u32[]{:S(2)}, u32[]{:S(2)}) %collective-permute-start.2) | collective-permute-done | bytes 65568 | tf_op jit(solution)/shard_map/ppermute | solution.py:355
  14.9 0.0 collective-permute-done.1.near_ref
  14.9 0.6 %shard_map.67 = (f32[8,128]{1,0:T(8,128)S(1)}, f32[8,128]{1,0:T(8,128)S(1)}, f32[8,128]{1,0:T(8,128)S(1)}) custom-call(bf16[128,256]{1,0:T(8,128)(2,1)S(1)} %shard_map.66.own_ref, bf16[128,256]{1,0:T(8,128)(2,1)S(1)} %collective-permute-done.1.near_ref, bf16[128,256]{1,0:T(8,128)(2,1)S(1)} %collective-permute-done.2.far_ref, ...), custom_call_target="tpu_custom_call" | custom-call | tf_op jit(solution)/shard_map/pallas_call | solution.py:291
  15.5 1.2 %collective-permute-start.4 = (f32[8,128]{1,0:T(8,128)S(1)}, f32[8,128]{1,0:T(8,128)S(1)}, u32[]{:S(2)}, u32[]{:S(2)}) collective-permute-start(f32[8,128]{1,0:T(8,128)S(1)} %get-tuple-element.23), channel_id=1, source_target_pairs={{0,3},{1,2},{2,1},{3,0},{4,7},{5,6},{6,5},{7,4},{8,11},{9,10},{10,... | collective-permute-start | bytes 12296 | tf_op jit(solution)/shard_map/ppermute | solution.py:342
  16.7 1.8 %collective-permute-start.5 = (f32[8,128]{1,0:T(8,128)S(1)}, f32[8,128]{1,0:T(8,128)S(1)}, u32[]{:S(2)}, u32[]{:S(2)}) collective-permute-start(f32[8,128]{1,0:T(8,128)S(1)} %get-tuple-element.24), channel_id=1, source_target_pairs={{0,9},{1,8},{2,11},{3,10},{4,13},{5,12},{6,15},{7,14},{9,4},{8,5},... | collective-permute-start | bytes 12296 | tf_op jit(solution)/shard_map/ppermute | solution.py:355
  18.5 0.1 collective-permute-done.4.got_ref
  18.6 3.0 %collective-permute-done.5.back_ref = f32[8,128]{1,0:T(8,128)S(1)} collective-permute-done((f32[8,128]{1,0:T(8,128)S(1)}, f32[8,128]{1,0:T(8,128)S(1)}, u32[]{:S(2)}, u32[]{:S(2)}) %collective-permute-start.5) | collective-permute-done | bytes 4128 | tf_op jit(solution)/shard_map/ppermute | solution.py:355
  21.6 0.1 shard_map.68
  21.7 0.4 %collective-permute-start.6 = (f32[4,128]{1,0:T(4,128)S(1)}, f32[4,128]{1,0:T(4,128)S(1)}, u32[]{:S(2)}, u32[]{:S(2)}) collective-permute-start(f32[4,128]{1,0:T(4,128)S(1)} %get-tuple-element.26), channel_id=1, source_target_pairs={{0,1},{1,0},{2,3},{3,2},{4,5},{5,4},{6,7},{7,6},{8,9},{9,8},{10,11... | collective-permute-start | bytes 6152 | tf_op jit(solution)/shard_map/ppermute | solution.py:338
  22.1 0.8 %collective-permute-done.6.got_ref = f32[4,128]{1,0:T(4,128)S(1)} collective-permute-done((f32[4,128]{1,0:T(4,128)S(1)}, f32[4,128]{1,0:T(4,128)S(1)}, u32[]{:S(2)}, u32[]{:S(2)}) %collective-permute-start.6) | collective-permute-done | bytes 2080 | tf_op jit(solution)/shard_map/ppermute | solution.py:338
  22.9 0.6 %shard_map.69 = f32[4,64]{1,0:T(4,128)} custom-call(f32[4,128]{1,0:T(4,128)S(1)} %get-tuple-element.25.keep_ref, f32[4,128]{1,0:T(4,128)S(1)} %collective-permute-done.6.got_ref), custom_call_target="tpu_custom_call" | custom-call | tf_op jit(solution)/shard_map/pallas_call | solution.py:328
Async XLA Ops:
  3.1 1.8 %collective-permute-start = (bf16[304,512]{1,0:T(8,128)(2,1)S(1)}, bf16[304,512]{1,0:T(8,128)(2,1)S(1)}, u32[]{:S(2)}, u32[]{:S(2)}) collective-permute-start(bf16[304,512]{1,0:T(8,128)(2,1)S(1)} %get-tuple-element.21), channel_id=1, source_target_pairs={{0,1},{1,0},{2,3},{3,2},{4,5},{5,4},{6,7},{7,6},{8,9},{9,8},{10,11... | collective-permute-start | bytes 933896 | tf_op jit(solution)/shard_map/ppermute | solution.py:338
  5.3 6.4 %collective-permute-start.3 = (bf16[128,256]{1,0:T(8,128)(2,1)S(1)}, bf16[128,256]{1,0:T(8,128)(2,1)S(1)}, u32[]{:S(2)}, u32[]{:S(2)}) collective-permute-start(bf16[128,256]{1,0:T(8,128)(2,1)S(1)} %shard_map.66.own_ref), channel_id=1, source_target_pairs={{0,4},{1,5},{2,6},{3,7},{4,0},{5,1},{6,2},{7,3},{9,13},{8,12},{11,... | collective-permute-start | bytes 196616 | tf_op jit(solution)/shard_map/ppermute | solution.py:355
  8.3 6.6 %collective-permute-start.2 = (bf16[128,256]{1,0:T(8,128)(2,1)S(1)}, bf16[128,256]{1,0:T(8,128)(2,1)S(1)}, u32[]{:S(2)}, u32[]{:S(2)}) collective-permute-start(bf16[128,256]{1,0:T(8,128)(2,1)S(1)} %shard_map.66.own_ref), channel_id=1, source_target_pairs={{0,13},{1,12},{2,15},{3,14},{4,9},{5,8},{6,11},{7,10},{9,0},{8,1},... | collective-permute-start | bytes 196616 | tf_op jit(solution)/shard_map/ppermute | solution.py:355
  10.2 4.7 %collective-permute-start.1 = (bf16[128,256]{1,0:T(8,128)(2,1)S(1)}, bf16[128,256]{1,0:T(8,128)(2,1)S(1)}, u32[]{:S(2)}, u32[]{:S(2)}) collective-permute-start(bf16[128,256]{1,0:T(8,128)(2,1)S(1)} %shard_map.66.own_ref), channel_id=1, source_target_pairs={{0,2},{2,0},{1,3},{3,1},{4,6},{6,4},{5,7},{7,5},{8,10},{10,8},{9,1... | collective-permute-start | bytes 196616 | tf_op jit(solution)/shard_map/ppermute | solution.py:346
  15.5 3.1 %collective-permute-start.4 = (f32[8,128]{1,0:T(8,128)S(1)}, f32[8,128]{1,0:T(8,128)S(1)}, u32[]{:S(2)}, u32[]{:S(2)}) collective-permute-start(f32[8,128]{1,0:T(8,128)S(1)} %get-tuple-element.23), channel_id=1, source_target_pairs={{0,3},{1,2},{2,1},{3,0},{4,7},{5,6},{6,5},{7,4},{8,11},{9,10},{10,... | collective-permute-start | bytes 12296 | tf_op jit(solution)/shard_map/ppermute | solution.py:342
  16.7 4.8 %collective-permute-start.5 = (f32[8,128]{1,0:T(8,128)S(1)}, f32[8,128]{1,0:T(8,128)S(1)}, u32[]{:S(2)}, u32[]{:S(2)}) collective-permute-start(f32[8,128]{1,0:T(8,128)S(1)} %get-tuple-element.24), channel_id=1, source_target_pairs={{0,9},{1,8},{2,11},{3,10},{4,13},{5,12},{6,15},{7,14},{9,4},{8,5},... | collective-permute-start | bytes 12296 | tf_op jit(solution)/shard_map/ppermute | solution.py:355
  21.7 1.2 %collective-permute-start.6 = (f32[4,128]{1,0:T(4,128)S(1)}, f32[4,128]{1,0:T(4,128)S(1)}, u32[]{:S(2)}, u32[]{:S(2)}) collective-permute-start(f32[4,128]{1,0:T(4,128)S(1)} %get-tuple-element.26), channel_id=1, source_target_pairs={{0,1},{1,0},{2,3},{3,2},{4,5},{5,4},{6,7},{7,6},{8,9},{9,8},{10,11... | collective-permute-start | bytes 6152 | tf_op jit(solution)/shard_map/ppermute | solution.py:338

commit v3 on v1

--- a/solution.py
+++ b/solution.py
@@ -91,14 +91,15 @@
 ):
     tokens, width = far.shape
     kind = kind_of(cross)
-    parts = 4
-    share = width // parts
     wide = BLOCK[1]
+    share = width // 4
+    ends = [0, share, 2 * share, 3 * share, width - wide, width]
+    parts = len(ends) - 1
 
     def copies(inputs, factor, factor_held, held, first):
         out = [pltpu.make_async_copy(factor, factor_held, sems.at[first])]
         for i in range(parts):
-            cols = pl.ds(i * share, share)
+            cols = pl.ds(ends[i], ends[i + 1] - ends[i])
             out.append(
                 pltpu.make_async_copy(inputs.at[:, cols], held.at[:, cols], sems.at[first + 1 + i])
             )
@@ -114,6 +115,7 @@
     salts_copy = pltpu.make_async_copy(salts_hbm, salts, sems.at[0])
     mask_copy = pltpu.make_async_copy(mask_hbm, mask, sems.at[1])
     salts_copy.start()
+    mask_copy.start()
 
     @pl.when(kind == 0)
     def _():
@@ -123,28 +125,12 @@
     def _():
         start_copies(cot_hbm, up_hbm, hid_hbm, down_hbm)
 
-    mask_copy.start()
     far_waits = copies(hid_hbm, down_hbm, far_factor, far, 2)
     near_waits = copies(hid_hbm, down_hbm, near_factor, near_ref, parts + 3)
     first = lax.axis_index("tensor") * int32_wrap(width * PROJ_ROWS * INDEX_MUL)
     start = table_start() + first
     salts_copy.wait()
     far_start = start + salts[2 - 2 * kind] * SALT_MUL
-    far_waits[0].wait()
-    near_waits[0].wait()
-    total = ranks = None
-    for col in range(0, width, wide):
-        part = slice(col, col + wide)
-        left = jnp.concatenate(sign_rows(far_start, col) + [far_factor[:, part]], axis=0)
-        if col % share == 0:
-            far_waits[1 + col // share].wait()
-            near_waits[1 + col // share].wait()
-        term = lax.dot_general(left, far[:, part], NT, preferred_element_type=F32)
-        total = term if total is None else total + term
-        term = lax.dot_general(
-            near_factor[:, part], near_ref[:, part], NT, preferred_element_type=F32
-        )
-        ranks = term if ranks is None else ranks + term
     start_ref[...] = start + salts[2 * kind] * SALT_MUL
     shape = mixer_ref.shape
     mixed, rank = iota(shape, 0) // ex_rows, iota(shape, 1) % ADAPTER_RANK
@@ -155,6 +141,21 @@
     far_kept = counted | (kind == 0)
     near_kept = counted | (kind == 1)
     kept_ref[...] = jnp.broadcast_to(jnp.where(near_kept, 1.0, 0.0), kept_ref.shape)
+    far_waits[0].wait()
+    near_waits[0].wait()
+    total = ranks = None
+    for col in range(0, width, wide):
+        part = slice(col, col + wide)
+        left = jnp.concatenate(sign_rows(far_start, col) + [far_factor[:, part]], axis=0)
+        if col in ends:
+            far_waits[1 + ends.index(col)].wait()
+            near_waits[1 + ends.index(col)].wait()
+        term = lax.dot_general(left, far[:, part], NT, preferred_element_type=F32)
+        total = term if total is None else total + term
+        term = lax.dot_general(
+            near_factor[:, part], near_ref[:, part], NT, preferred_element_type=F32
+        )
+        ranks = term if ranks is None else ranks + term
     total = jnp.where(far_kept, total, 0.0)
     send_ref[:PROJ_ROWS] = total[:PROJ_ROWS].astype(BF16)
     ranks_ref[...] = split_pieces(total[PROJ_ROWS:])
@@ -184,7 +185,7 @@
             pltpu.VMEM((ADAPTER_RANK, width), BF16),
             pltpu.VMEM((ADAPTER_RANK, width), BF16),
             pltpu.VMEM((tokens, width), BF16),
-            pltpu.SemaphoreType.DMA((12,)),
+            pltpu.SemaphoreType.DMA((14,)),
         ],
         compiler_params=SMALL,
     )(*[pltpu.with_memory_space_constraint(x, pltpu.HBM) for x in arrays])
@@ -260,9 +261,10 @@
     for row in range(0, near_ref.shape[0], wide):
         part = slice(row, row + wide)
         left = jnp.concatenate([z_refs[0][part, :], near_ref[part, :]], axis=0)
-        right = jnp.concatenate([ref[part, :] for ref in z_refs] * 2, axis=0)
+        right = jnp.concatenate([ref[part, :] for ref in z_refs], axis=0)
         term = lax.dot_general(left, right, NT, preferred_element_type=F32)
         total = term if total is None else total + term
+    total = jnp.concatenate([total, total], axis=1)
     keep_ref[...] = order_blocks(fold_ranks(total[:wide]), wide)
     send_ref[...] = order_blocks(fold_ranks(total[wide:]), wide)
 

time: 21.5 us -> 21.4 us (level)
  no operation moved by 1% of the time
where the time goes in v3:
time: 21.4 us; the launch traced here: 21.3 us
  starting transfers between devices  8.93 us (42%)
  waiting for transfers between devices  6.75 us (32%)
  Pallas kernels  5.55 us (26%)
    ppermute x3, starting transfers between devices, swap_z(): lax.ppermute(value, BLK + ('tensor',), [(i, i ^ other) for i in range(16)])  5.43 us
    ppermute x3, waiting for transfers between devices, swap_z(): lax.ppermute(value, BLK + ('tensor',), [(i, i ^ other) for i in range(16)])  3.71 us
    pallas_call x1, Pallas kernels, far_rows(): pl.pallas_call(functools.partial(far_kernel, cross, ex_rows), out_shape=[...  3.05 us
    ppermute x1, waiting for transfers between devices, swap_across(): return lax.ppermute(value, ('x', 'tensor'), [(i, i ^ 3) for i in range(4)])  1.81 us
    ppermute x1, starting transfers between devices, swap_x(): return lax.ppermute(value, 'x', [(0, 1), (1, 0)])  1.6 us
    ppermute x1, starting transfers between devices, swap_across(): return lax.ppermute(value, ('x', 'tensor'), [(i, i ^ 3) for i in range(4)])  1.25 us
    ppermute x2, waiting for transfers between devices, swap_cores(): return lax.ppermute(value, 'tensor', [(0, 1), (1, 0)])  1.23 us
    pallas_call x1, Pallas kernels, near_rows(): pl.pallas_call(near_kernel, out_shape=jax.ShapeDtypeStruct((PROJ_ROWS, to...  1.02 us
  transfers between devices with their start and end apart: 7, of which 5 were waited for; matrix products, arithmetic and copies ran while one was open for 0% of the time, Pallas kernels for 5%

profile of v3, /device:TPU:0, one launch (start us, length us, event | category | flops | bytes accessed | tf_op | source)
XLA Modules:
  0.0 21.3 jit_solution(5975070671520098333)
XLA Ops:
  0.0 3.0 %shard_map.64 = (bf16[304,512]{1,0:T(8,128)(2,1)S(1)}, bf16[48,512]{1,0:T(8,128)(2,1)S(1)}, bf16[512,2048]{1,0:T(8,128)(2,1)S(1)}, s32[16,256]{1,0:T(8,128)S(1)}...) custom-call(s32[4]{0:T(128)} %salts_hbm.1, s32[8,64]{1,0:T(8,128)} %mask_hbm.1, bf16[16,2048]{1,0:T(8,128)(2,1)} %down_hbm.1, ...), custom_call_target="tpu_custom_call" | custom-call | tf_op jit(solution)/shard_map/pallas_call | solution.py:170
  3.1 0.5 %collective-permute-start = (bf16[304,512]{1,0:T(8,128)(2,1)S(1)}, bf16[304,512]{1,0:T(8,128)(2,1)S(1)}, u32[]{:S(2)}, u32[]{:S(2)}) collective-permute-start(bf16[304,512]{1,0:T(8,128)(2,1)S(1)} %get-tuple-element.20), channel_id=1, source_target_pairs={{0,1},{1,0},{2,3},{3,2},{4,5},{5,4},{6,7},{7,6},{8,9},{9,8},{10,11... | collective-permute-start | bytes 933896 | tf_op jit(solution)/shard_map/ppermute | solution.py:320
  3.6 1.0 %shard_map.65.own_ref = bf16[256,512]{1,0:T(8,128)(2,1)S(1)} custom-call(s32[16,256]{1,0:T(8,128)S(1)} %get-tuple-element.17.start_ref, f32[8,512]{1,0:T(8,128)S(1)} %get-tuple-element.18.kept_ref, bf16[512,2048]{1,0:T(8,128)(2,1)S(1)} %get-tuple-element.19.near_ref), custom_call_target="tpu_custom_call" | custom-call | flops 536870912 | bytes 2097152 | tf_op jit(solution)/shard_map/pallas_call | solution.py:209
  4.6 0.2 %collective-permute-done.other_ref = bf16[304,512]{1,0:T(8,128)(2,1)S(1)} collective-permute-done((bf16[304,512]{1,0:T(8,128)(2,1)S(1)}, bf16[304,512]{1,0:T(8,128)(2,1)S(1)}, u32[]{:S(2)}, u32[]{:S(2)}) %collective-permute-start) | collective-permute-done | bytes 311328 | tf_op jit(solution)/shard_map/ppermute | solution.py:320
  4.8 0.4 %shard_map.66.refs_0_ = bf16[128,256]{1,0:T(8,128)(2,1)S(1)} custom-call(bf16[128,96]{1,0:T(8,128)(2,1)S(1)} %get-tuple-element.15.mixer_ref, bf16[48,512]{1,0:T(8,128)(2,1)S(1)} %get-tuple-element.16.ranks_ref, bf16[256,512]{1,0:T(8,128)(2,1)S(1)} %shard_map.65.own_ref, bf16[304,512]{1,0:T(8,128)(2,1)S(1)} %collective-permute-done.other_ref), custom_call_target="tpu_custom_call" | custom-call | tf_op jit(solution)/shard_map/pallas_call | solution.py:234
  5.2 4.8 %collective-permute-start.4 = (bf16[128,256]{1,0:T(8,128)(2,1)S(1)}, bf16[128,256]{1,0:T(8,128)(2,1)S(1)}, u32[]{:S(2)}, u32[]{:S(2)}) collective-permute-start(bf16[128,256]{1,0:T(8,128)(2,1)S(1)} %shard_map.66.refs_0_), channel_id=1, source_target_pairs={{0,13},{1,12},{2,15},{3,14},{4,9},{5,8},{6,11},{7,10},{8,5},{9,4},... | collective-permute-start | bytes 196616 | tf_op jit(solution)/shard_map/ppermute | solution.py:333
  10.0 0.0 collective-permute-start.3
  10.0 0.7 %collective-permute-start.2 = (bf16[128,256]{1,0:T(8,128)(2,1)S(1)}, bf16[128,256]{1,0:T(8,128)(2,1)S(1)}, u32[]{:S(2)}, u32[]{:S(2)}) collective-permute-start(bf16[128,256]{1,0:T(8,128)(2,1)S(1)} %shard_map.66.refs_0_), channel_id=1, source_target_pairs={{0,4},{1,5},{2,6},{3,7},{4,0},{5,1},{6,2},{7,3},{8,12},{9,13},{10,... | collective-permute-start | bytes 196616 | tf_op jit(solution)/shard_map/ppermute | solution.py:333
  10.6 1.6 %collective-permute-start.1 = (bf16[128,256]{1,0:T(8,128)(2,1)S(1)}, bf16[128,256]{1,0:T(8,128)(2,1)S(1)}, u32[]{:S(2)}, u32[]{:S(2)}) collective-permute-start(bf16[128,256]{1,0:T(8,128)(2,1)S(1)} %shard_map.66.refs_0_), channel_id=1, source_target_pairs={{0,2},{2,0},{1,3},{3,1},{4,6},{6,4},{5,7},{7,5},{8,10},{10,8},{9,1... | collective-permute-start | bytes 196616 | tf_op jit(solution)/shard_map/ppermute | solution.py:328
  12.2 0.3 %collective-permute-done.4.refs_3_ = bf16[128,256]{1,0:T(8,128)(2,1)S(1)} collective-permute-done((bf16[128,256]{1,0:T(8,128)(2,1)S(1)}, bf16[128,256]{1,0:T(8,128)(2,1)S(1)}, u32[]{:S(2)}, u32[]{:S(2)}) %collective-permute-start.4) | collective-permute-done | bytes 65568 | tf_op jit(solution)/shard_map/ppermute | solution.py:333
  12.5 3.4 %collective-permute-done.3.refs_2_ = bf16[128,256]{1,0:T(8,128)(2,1)S(1)} collective-permute-done((bf16[128,256]{1,0:T(8,128)(2,1)S(1)}, bf16[128,256]{1,0:T(8,128)(2,1)S(1)}, u32[]{:S(2)}, u32[]{:S(2)}) %collective-permute-start.3) | collective-permute-done | bytes 65568 | tf_op jit(solution)/shard_map/ppermute | solution.py:333
  15.9 0.0 collective-permute-done.2.refs_1_
  15.9 0.0 collective-permute-done.1.near_ref
  15.9 0.5 %shard_map.67 = (f32[8,128]{1,0:T(8,128)S(1)}, f32[8,128]{1,0:T(8,128)S(1)}) custom-call(bf16[128,256]{1,0:T(8,128)(2,1)S(1)} %collective-permute-done.1.near_ref, bf16[128,256]{1,0:T(8,128)(2,1)S(1)} %shard_map.66.refs_0_, bf16[128,256]{1,0:T(8,128)(2,1)S(1)} %collective-permute-done.2.refs_1_, bf16[128,256]{1,0:T(8,128)(2,1)S(1)} %collective-permute-done.3.refs_2_, ...), custom_call_target="tpu_custom_call" | custom-call | tf_op jit(solution)/shard_map/pallas_call | solution.py:273
  16.4 1.2 %collective-permute-start.5 = (f32[8,128]{1,0:T(8,128)S(1)}, f32[8,128]{1,0:T(8,128)S(1)}, u32[]{:S(2)}, u32[]{:S(2)}) collective-permute-start(f32[8,128]{1,0:T(8,128)S(1)} %get-tuple-element.22), channel_id=1, source_target_pairs={{0,3},{1,2},{2,1},{3,0},{4,7},{5,6},{6,5},{7,4},{8,11},{9,10},{10,... | collective-permute-start | bytes 12296 | tf_op jit(solution)/shard_map/ppermute | solution.py:324
  17.6 1.8 %collective-permute-done.5.got_ref = f32[8,128]{1,0:T(8,128)S(1)} collective-permute-done((f32[8,128]{1,0:T(8,128)S(1)}, f32[8,128]{1,0:T(8,128)S(1)}, u32[]{:S(2)}, u32[]{:S(2)}) %collective-permute-start.5) | collective-permute-done | bytes 4128 | tf_op jit(solution)/shard_map/ppermute | solution.py:324
  19.4 0.1 shard_map.68
  19.5 0.1 collective-permute-start.6
  19.7 1.0 %collective-permute-done.6.got_ref = f32[4,128]{1,0:T(4,128)S(1)} collective-permute-done((f32[4,128]{1,0:T(4,128)S(1)}, f32[4,128]{1,0:T(4,128)S(1)}, u32[]{:S(2)}, u32[]{:S(2)}) %collective-permute-start.6) | collective-permute-done | bytes 2080 | tf_op jit(solution)/shard_map/ppermute | solution.py:320
  20.7 0.6 %shard_map.69 = f32[4,64]{1,0:T(4,128)} custom-call(f32[4,128]{1,0:T(4,128)S(1)} %get-tuple-element.23.keep_ref, f32[4,128]{1,0:T(4,128)S(1)} %collective-permute-done.6.got_ref), custom_call_target="tpu_custom_call" | custom-call | tf_op jit(solution)/shard_map/pallas_call | solution.py:310
Async XLA Ops:
  3.1 1.7 %collective-permute-start = (bf16[304,512]{1,0:T(8,128)(2,1)S(1)}, bf16[304,512]{1,0:T(8,128)(2,1)S(1)}, u32[]{:S(2)}, u32[]{:S(2)}) collective-permute-start(bf16[304,512]{1,0:T(8,128)(2,1)S(1)} %get-tuple-element.20), channel_id=1, source_target_pairs={{0,1},{1,0},{2,3},{3,2},{4,5},{5,4},{6,7},{7,6},{8,9},{9,8},{10,11... | collective-permute-start | bytes 933896 | tf_op jit(solution)/shard_map/ppermute | solution.py:320
  5.2 7.3 %collective-permute-start.4 = (bf16[128,256]{1,0:T(8,128)(2,1)S(1)}, bf16[128,256]{1,0:T(8,128)(2,1)S(1)}, u32[]{:S(2)}, u32[]{:S(2)}) collective-permute-start(bf16[128,256]{1,0:T(8,128)(2,1)S(1)} %shard_map.66.refs_0_), channel_id=1, source_target_pairs={{0,13},{1,12},{2,15},{3,14},{4,9},{5,8},{6,11},{7,10},{8,5},{9,4},... | collective-permute-start | bytes 196616 | tf_op jit(solution)/shard_map/ppermute | solution.py:333
  10.0 6.0 %collective-permute-start.3 = (bf16[128,256]{1,0:T(8,128)(2,1)S(1)}, bf16[128,256]{1,0:T(8,128)(2,1)S(1)}, u32[]{:S(2)}, u32[]{:S(2)}) collective-permute-start(bf16[128,256]{1,0:T(8,128)(2,1)S(1)} %shard_map.66.refs_0_), channel_id=1, source_target_pairs={{0,9},{1,8},{2,11},{3,10},{4,13},{5,12},{6,15},{7,14},{8,1},{9,0},... | collective-permute-start | bytes 196616 | tf_op jit(solution)/shard_map/ppermute | solution.py:333
  10.0 6.0 %collective-permute-start.2 = (bf16[128,256]{1,0:T(8,128)(2,1)S(1)}, bf16[128,256]{1,0:T(8,128)(2,1)S(1)}, u32[]{:S(2)}, u32[]{:S(2)}) collective-permute-start(bf16[128,256]{1,0:T(8,128)(2,1)S(1)} %shard_map.66.refs_0_), channel_id=1, source_target_pairs={{0,4},{1,5},{2,6},{3,7},{4,0},{5,1},{6,2},{7,3},{8,12},{9,13},{10,... | collective-permute-start | bytes 196616 | tf_op jit(solution)/shard_map/ppermute | solution.py:333
  10.6 5.3 %collective-permute-start.1 = (bf16[128,256]{1,0:T(8,128)(2,1)S(1)}, bf16[128,256]{1,0:T(8,128)(2,1)S(1)}, u32[]{:S(2)}, u32[]{:S(2)}) collective-permute-start(bf16[128,256]{1,0:T(8,128)(2,1)S(1)} %shard_map.66.refs_0_), channel_id=1, source_target_pairs={{0,2},{2,0},{1,3},{3,1},{4,6},{6,4},{5,7},{7,5},{8,10},{10,8},{9,1... | collective-permute-start | bytes 196616 | tf_op jit(solution)/shard_map/ppermute | solution.py:328
  16.4 3.1 %collective-permute-start.5 = (f32[8,128]{1,0:T(8,128)S(1)}, f32[8,128]{1,0:T(8,128)S(1)}, u32[]{:S(2)}, u32[]{:S(2)}) collective-permute-start(f32[8,128]{1,0:T(8,128)S(1)} %get-tuple-element.22), channel_id=1, source_target_pairs={{0,3},{1,2},{2,1},{3,0},{4,7},{5,6},{6,5},{7,4},{8,11},{9,10},{10,... | collective-permute-start | bytes 12296 | tf_op jit(solution)/shard_map/ppermute | solution.py:324
  19.5 1.2 %collective-permute-start.6 = (f32[4,128]{1,0:T(4,128)S(1)}, f32[4,128]{1,0:T(4,128)S(1)}, u32[]{:S(2)}, u32[]{:S(2)}) collective-permute-start(f32[4,128]{1,0:T(4,128)S(1)} %get-tuple-element.24), channel_id=1, source_target_pairs={{0,1},{1,0},{2,3},{3,2},{4,5},{5,4},{6,7},{7,6},{8,9},{9,8},{10,11... | collective-permute-start | bytes 6152 | tf_op jit(solution)/shard_map/ppermute | solution.py:320

commit v4 on v3

--- a/solution.py
+++ b/solution.py
@@ -254,8 +254,8 @@
     return jnp.where((z & 1) != 0, swapped, rows)
 
 
-def pair_kernel(ex_rows, near_ref, *refs):
-    *z_refs, keep_ref, send_ref = refs
+def pair_kernel(ex_rows, near_ref, own_ref, first_ref, third_ref, second_ref, keep_ref, send_ref):
+    z_refs = (own_ref, first_ref, second_ref, third_ref)
     wide = 2 * ex_rows
     total = None
     for row in range(0, near_ref.shape[0], wide):
@@ -269,14 +269,14 @@
     send_ref[...] = order_blocks(fold_ranks(total[wide:]), wide)
 
 
-def pair_rows(near, by_z, ex_rows):
+def pair_rows(near, own, first, third, second, ex_rows):
     return pl.pallas_call(
         functools.partial(pair_kernel, ex_rows),
         out_shape=[jax.ShapeDtypeStruct((ex_rows, LANES), F32)] * 2,
-        in_specs=[VMEM] * (1 + len(by_z)),
+        in_specs=[VMEM] * 5,
         out_specs=[VMEM] * 2,
         compiler_params=SMALL,
-    )(near, *by_z)
+    )(near, own, first, third, second)
 
 
 def halves_kernel(own_ref, got_ref, keep_ref, send_ref):
@@ -352,11 +352,11 @@
     terms = (mixer, ranks, near_rows(start, kept, near), other)
     features = feature_rows(*terms, ex_rows)
     if fast:
+        second = swap_z(features, 2)
         third = swap_z(features, 3)
-        second = swap_z(features, 2)
         first = swap_z(features, 1)
         near = swap_x(features)
-        keep, send = pair_rows(near, (features, first, second, third), ex_rows)
+        keep, send = pair_rows(near, features, first, third, second, ex_rows)
         keep, send = join_halves(keep, swap_across(send))
         return sum_rows(keep, swap_cores(send))
     share = ADAPTER_RANK * PROJ_ROWS // blocks

time: 21.4 us -> 21.4 us (level)
  waiting for transfers between devices: 6.75 us -> 7.29 us
  starting transfers between devices: 8.93 us -> 8.4 us
    ppermute x1, starting transfers between devices: 1.25 us -> 0.92 us  [swap_across(): return lax.ppermute(value, ('x', 'tensor'), [(i, i ^ 3) for i in range(4)])]
    ppermute x1, waiting for transfers between devices: 1.81 us -> 2.14 us  [swap_across(): return lax.ppermute(value, ('x', 'tensor'), [(i, i ^ 3) for i in range(4)])]
where the time goes in v4:
time: 21.4 us; the launch traced here: 21.3 us
  starting transfers between devices  8.4 us (39%)
  waiting for transfers between devices  7.29 us (34%)
  Pallas kernels  5.55 us (26%)
    ppermute x3, starting transfers between devices, swap_z(): lax.ppermute(value, BLK + ('tensor',), [(i, i ^ other) for i in range(16)])  5.35 us
    ppermute x3, waiting for transfers between devices, swap_z(): lax.ppermute(value, BLK + ('tensor',), [(i, i ^ other) for i in range(16)])  3.9 us
    pallas_call x1, Pallas kernels, far_rows(): pl.pallas_call(functools.partial(far_kernel, cross, ex_rows), out_shape=[...  3.05 us
    ppermute x1, waiting for transfers between devices, swap_across(): return lax.ppermute(value, ('x', 'tensor'), [(i, i ^ 3) for i in range(4)])  2.14 us
    ppermute x1, starting transfers between devices, swap_x(): return lax.ppermute(value, 'x', [(0, 1), (1, 0)])  1.5 us
    ppermute x2, waiting for transfers between devices, swap_cores(): return lax.ppermute(value, 'tensor', [(0, 1), (1, 0)])  1.25 us
    pallas_call x1, Pallas kernels, near_rows(): pl.pallas_call(near_kernel, out_shape=jax.ShapeDtypeStruct((PROJ_ROWS, to...  1.02 us
    ppermute x1, starting transfers between devices, swap_across(): return lax.ppermute(value, ('x', 'tensor'), [(i, i ^ 3) for i in range(4)])  0.92 us
  transfers between devices with their start and end apart: 7, of which 5 were waited for; matrix products, arithmetic and copies ran while one was open for 0% of the time, Pallas kernels for 5%

profile of v4, /device:TPU:0, one launch (start us, length us, event | category | flops | bytes accessed | tf_op | source)
XLA Modules:
  0.0 21.3 jit_solution(8844647270729650280)
XLA Ops:
  0.0 3.0 %shard_map.64 = (bf16[304,512]{1,0:T(8,128)(2,1)S(1)}, bf16[48,512]{1,0:T(8,128)(2,1)S(1)}, bf16[512,2048]{1,0:T(8,128)(2,1)S(1)}, s32[16,256]{1,0:T(8,128)S(1)}...) custom-call(s32[4]{0:T(128)} %salts_hbm.1, s32[8,64]{1,0:T(8,128)} %mask_hbm.1, bf16[16,2048]{1,0:T(8,128)(2,1)} %down_hbm.1, ...), custom_call_target="tpu_custom_call" | custom-call | tf_op jit(solution)/shard_map/pallas_call | solution.py:170
  3.1 0.5 %collective-permute-start = (bf16[304,512]{1,0:T(8,128)(2,1)S(1)}, bf16[304,512]{1,0:T(8,128)(2,1)S(1)}, u32[]{:S(2)}, u32[]{:S(2)}) collective-permute-start(bf16[304,512]{1,0:T(8,128)(2,1)S(1)} %get-tuple-element.20), channel_id=1, source_target_pairs={{0,1},{1,0},{2,3},{3,2},{4,5},{5,4},{6,7},{7,6},{8,9},{9,8},{10,11... | collective-permute-start | bytes 933896 | tf_op jit(solution)/shard_map/ppermute | solution.py:320
  3.6 1.0 %shard_map.65.own_ref = bf16[256,512]{1,0:T(8,128)(2,1)S(1)} custom-call(s32[16,256]{1,0:T(8,128)S(1)} %get-tuple-element.17.start_ref, f32[8,512]{1,0:T(8,128)S(1)} %get-tuple-element.18.kept_ref, bf16[512,2048]{1,0:T(8,128)(2,1)S(1)} %get-tuple-element.19.near_ref), custom_call_target="tpu_custom_call" | custom-call | flops 536870912 | bytes 2097152 | tf_op jit(solution)/shard_map/pallas_call | solution.py:209
  4.6 0.2 %collective-permute-done.other_ref = bf16[304,512]{1,0:T(8,128)(2,1)S(1)} collective-permute-done((bf16[304,512]{1,0:T(8,128)(2,1)S(1)}, bf16[304,512]{1,0:T(8,128)(2,1)S(1)}, u32[]{:S(2)}, u32[]{:S(2)}) %collective-permute-start) | collective-permute-done | bytes 311328 | tf_op jit(solution)/shard_map/ppermute | solution.py:320
  4.8 0.4 %shard_map.66.own_ref = bf16[128,256]{1,0:T(8,128)(2,1)S(1)} custom-call(bf16[128,96]{1,0:T(8,128)(2,1)S(1)} %get-tuple-element.15.mixer_ref, bf16[48,512]{1,0:T(8,128)(2,1)S(1)} %get-tuple-element.16.ranks_ref, bf16[256,512]{1,0:T(8,128)(2,1)S(1)} %shard_map.65.own_ref, bf16[304,512]{1,0:T(8,128)(2,1)S(1)} %collective-permute-done.other_ref), custom_call_target="tpu_custom_call" | custom-call | tf_op jit(solution)/shard_map/pallas_call | solution.py:234
  5.2 3.8 %collective-permute-start.4 = (bf16[128,256]{1,0:T(8,128)(2,1)S(1)}, bf16[128,256]{1,0:T(8,128)(2,1)S(1)}, u32[]{:S(2)}, u32[]{:S(2)}) collective-permute-start(bf16[128,256]{1,0:T(8,128)(2,1)S(1)} %shard_map.66.own_ref), channel_id=1, source_target_pairs={{0,9},{1,8},{2,11},{3,10},{4,13},{5,12},{6,15},{7,14},{8,1},{9,0},... | collective-permute-start | bytes 196616 | tf_op jit(solution)/shard_map/ppermute | solution.py:333
  8.9 1.3 %collective-permute-start.3 = (bf16[128,256]{1,0:T(8,128)(2,1)S(1)}, bf16[128,256]{1,0:T(8,128)(2,1)S(1)}, u32[]{:S(2)}, u32[]{:S(2)}) collective-permute-start(bf16[128,256]{1,0:T(8,128)(2,1)S(1)} %shard_map.66.own_ref), channel_id=1, source_target_pairs={{0,13},{1,12},{2,15},{3,14},{4,9},{5,8},{6,11},{7,10},{8,5},{9,4},... | collective-permute-start | bytes 196616 | tf_op jit(solution)/shard_map/ppermute | solution.py:333
  10.3 0.3 %collective-permute-start.2 = (bf16[128,256]{1,0:T(8,128)(2,1)S(1)}, bf16[128,256]{1,0:T(8,128)(2,1)S(1)}, u32[]{:S(2)}, u32[]{:S(2)}) collective-permute-start(bf16[128,256]{1,0:T(8,128)(2,1)S(1)} %shard_map.66.own_ref), channel_id=1, source_target_pairs={{0,4},{1,5},{2,6},{3,7},{4,0},{5,1},{6,2},{7,3},{8,12},{9,13},{10,... | collective-permute-start | bytes 196616 | tf_op jit(solution)/shard_map/ppermute | solution.py:333
  10.5 1.5 %collective-permute-start.1 = (bf16[128,256]{1,0:T(8,128)(2,1)S(1)}, bf16[128,256]{1,0:T(8,128)(2,1)S(1)}, u32[]{:S(2)}, u32[]{:S(2)}) collective-permute-start(bf16[128,256]{1,0:T(8,128)(2,1)S(1)} %shard_map.66.own_ref), channel_id=1, source_target_pairs={{0,2},{2,0},{1,3},{3,1},{4,6},{6,4},{5,7},{7,5},{8,10},{10,8},{9,1... | collective-permute-start | bytes 196616 | tf_op jit(solution)/shard_map/ppermute | solution.py:328
  12.0 0.0 collective-permute-done.4.second_ref
  12.0 2.8 %collective-permute-done.3.third_ref = bf16[128,256]{1,0:T(8,128)(2,1)S(1)} collective-permute-done((bf16[128,256]{1,0:T(8,128)(2,1)S(1)}, bf16[128,256]{1,0:T(8,128)(2,1)S(1)}, u32[]{:S(2)}, u32[]{:S(2)}) %collective-permute-start.3) | collective-permute-done | bytes 65568 | tf_op jit(solution)/shard_map/ppermute | solution.py:333
  14.9 1.1 %collective-permute-done.2.first_ref = bf16[128,256]{1,0:T(8,128)(2,1)S(1)} collective-permute-done((bf16[128,256]{1,0:T(8,128)(2,1)S(1)}, bf16[128,256]{1,0:T(8,128)(2,1)S(1)}, u32[]{:S(2)}, u32[]{:S(2)}) %collective-permute-start.2) | collective-permute-done | bytes 65568 | tf_op jit(solution)/shard_map/ppermute | solution.py:333
  15.9 0.0 collective-permute-done.1.near_ref
  15.9 0.5 %shard_map.67 = (f32[8,128]{1,0:T(8,128)S(1)}, f32[8,128]{1,0:T(8,128)S(1)}) custom-call(bf16[128,256]{1,0:T(8,128)(2,1)S(1)} %collective-permute-done.1.near_ref, bf16[128,256]{1,0:T(8,128)(2,1)S(1)} %shard_map.66.own_ref, bf16[128,256]{1,0:T(8,128)(2,1)S(1)} %collective-permute-done.2.first_ref, bf16[128,256]{1,0:T(8,128)(2,1)S(1)} %collective-permute-done.3.third_ref, ...), custom_call_target="tpu_custom_call" | custom-call | tf_op jit(solution)/shard_map/pallas_call | solution.py:273
  16.4 0.9 %collective-permute-start.5 = (f32[8,128]{1,0:T(8,128)S(1)}, f32[8,128]{1,0:T(8,128)S(1)}, u32[]{:S(2)}, u32[]{:S(2)}) collective-permute-start(f32[8,128]{1,0:T(8,128)S(1)} %get-tuple-element.22), channel_id=1, source_target_pairs={{0,3},{1,2},{2,1},{3,0},{4,7},{5,6},{6,5},{7,4},{8,11},{9,10},{10,... | collective-permute-start | bytes 12296 | tf_op jit(solution)/shard_map/ppermute | solution.py:324
  17.3 2.1 %collective-permute-done.5.got_ref = f32[8,128]{1,0:T(8,128)S(1)} collective-permute-done((f32[8,128]{1,0:T(8,128)S(1)}, f32[8,128]{1,0:T(8,128)S(1)}, u32[]{:S(2)}, u32[]{:S(2)}) %collective-permute-start.5) | collective-permute-done | bytes 4128 | tf_op jit(solution)/shard_map/ppermute | solution.py:324
  19.5 0.1 shard_map.68
  19.5 0.1 collective-permute-start.6
  19.6 1.0 %collective-permute-done.6.got_ref = f32[4,128]{1,0:T(4,128)S(1)} collective-permute-done((f32[4,128]{1,0:T(4,128)S(1)}, f32[4,128]{1,0:T(4,128)S(1)}, u32[]{:S(2)}, u32[]{:S(2)}) %collective-permute-start.6) | collective-permute-done | bytes 2080 | tf_op jit(solution)/shard_map/ppermute | solution.py:320
  20.7 0.6 %shard_map.69 = f32[4,64]{1,0:T(4,128)} custom-call(f32[4,128]{1,0:T(4,128)S(1)} %get-tuple-element.23.keep_ref, f32[4,128]{1,0:T(4,128)S(1)} %collective-permute-done.6.got_ref), custom_call_target="tpu_custom_call" | custom-call | tf_op jit(solution)/shard_map/pallas_call | solution.py:310
Async XLA Ops:
  3.1 1.7 %collective-permute-start = (bf16[304,512]{1,0:T(8,128)(2,1)S(1)}, bf16[304,512]{1,0:T(8,128)(2,1)S(1)}, u32[]{:S(2)}, u32[]{:S(2)}) collective-permute-start(bf16[304,512]{1,0:T(8,128)(2,1)S(1)} %get-tuple-element.20), channel_id=1, source_target_pairs={{0,1},{1,0},{2,3},{3,2},{4,5},{5,4},{6,7},{7,6},{8,9},{9,8},{10,11... | collective-permute-start | bytes 933896 | tf_op jit(solution)/shard_map/ppermute | solution.py:320
  5.2 6.9 %collective-permute-start.4 = (bf16[128,256]{1,0:T(8,128)(2,1)S(1)}, bf16[128,256]{1,0:T(8,128)(2,1)S(1)}, u32[]{:S(2)}, u32[]{:S(2)}) collective-permute-start(bf16[128,256]{1,0:T(8,128)(2,1)S(1)} %shard_map.66.own_ref), channel_id=1, source_target_pairs={{0,9},{1,8},{2,11},{3,10},{4,13},{5,12},{6,15},{7,14},{8,1},{9,0},... | collective-permute-start | bytes 196616 | tf_op jit(solution)/shard_map/ppermute | solution.py:333
  8.9 5.9 %collective-permute-start.3 = (bf16[128,256]{1,0:T(8,128)(2,1)S(1)}, bf16[128,256]{1,0:T(8,128)(2,1)S(1)}, u32[]{:S(2)}, u32[]{:S(2)}) collective-permute-start(bf16[128,256]{1,0:T(8,128)(2,1)S(1)} %shard_map.66.own_ref), channel_id=1, source_target_pairs={{0,13},{1,12},{2,15},{3,14},{4,9},{5,8},{6,11},{7,10},{8,5},{9,4},... | collective-permute-start | bytes 196616 | tf_op jit(solution)/shard_map/ppermute | solution.py:333
  10.3 5.7 %collective-permute-start.2 = (bf16[128,256]{1,0:T(8,128)(2,1)S(1)}, bf16[128,256]{1,0:T(8,128)(2,1)S(1)}, u32[]{:S(2)}, u32[]{:S(2)}) collective-permute-start(bf16[128,256]{1,0:T(8,128)(2,1)S(1)} %shard_map.66.own_ref), channel_id=1, source_target_pairs={{0,4},{1,5},{2,6},{3,7},{4,0},{5,1},{6,2},{7,3},{8,12},{9,13},{10,... | collective-permute-start | bytes 196616 | tf_op jit(solution)/shard_map/ppermute | solution.py:333
  10.5 5.4 %collective-permute-start.1 = (bf16[128,256]{1,0:T(8,128)(2,1)S(1)}, bf16[128,256]{1,0:T(8,128)(2,1)S(1)}, u32[]{:S(2)}, u32[]{:S(2)}) collective-permute-start(bf16[128,256]{1,0:T(8,128)(2,1)S(1)} %shard_map.66.own_ref), channel_id=1, source_target_pairs={{0,2},{2,0},{1,3},{3,1},{4,6},{6,4},{5,7},{7,5},{8,10},{10,8},{9,1... | collective-permute-start | bytes 196616 | tf_op jit(solution)/shard_map/ppermute | solution.py:328
  16.4 3.1 %collective-permute-start.5 = (f32[8,128]{1,0:T(8,128)S(1)}, f32[8,128]{1,0:T(8,128)S(1)}, u32[]{:S(2)}, u32[]{:S(2)}) collective-permute-start(f32[8,128]{1,0:T(8,128)S(1)} %get-tuple-element.22), channel_id=1, source_target_pairs={{0,3},{1,2},{2,1},{3,0},{4,7},{5,6},{6,5},{7,4},{8,11},{9,10},{10,... | collective-permute-start | bytes 12296 | tf_op jit(solution)/shard_map/ppermute | solution.py:324
  19.5 1.2 %collective-permute-start.6 = (f32[4,128]{1,0:T(4,128)S(1)}, f32[4,128]{1,0:T(4,128)S(1)}, u32[]{:S(2)}, u32[]{:S(2)}) collective-permute-start(f32[4,128]{1,0:T(4,128)S(1)} %get-tuple-element.24), channel_id=1, source_target_pairs={{0,1},{1,0},{2,3},{3,2},{4,5},{5,4},{6,7},{7,6},{8,9},{9,8},{10,11... | collective-permute-start | bytes 6152 | tf_op jit(solution)/shard_map/ppermute | solution.py:320

commit v5 on v4

--- a/solution.py
+++ b/solution.py
@@ -254,7 +254,7 @@
     return jnp.where((z & 1) != 0, swapped, rows)
 
 
-def pair_kernel(ex_rows, near_ref, own_ref, first_ref, third_ref, second_ref, keep_ref, send_ref):
+def pair_kernel(ex_rows, near_ref, own_ref, third_ref, first_ref, second_ref, keep_ref, send_ref):
     z_refs = (own_ref, first_ref, second_ref, third_ref)
     wide = 2 * ex_rows
     total = None
@@ -269,14 +269,14 @@
     send_ref[...] = order_blocks(fold_ranks(total[wide:]), wide)
 
 
-def pair_rows(near, own, first, third, second, ex_rows):
+def pair_rows(near, own, third, first, second, ex_rows):
     return pl.pallas_call(
         functools.partial(pair_kernel, ex_rows),
         out_shape=[jax.ShapeDtypeStruct((ex_rows, LANES), F32)] * 2,
         in_specs=[VMEM] * 5,
         out_specs=[VMEM] * 2,
         compiler_params=SMALL,
-    )(near, own, first, third, second)
+    )(near, own, third, first, second)
 
 
 def halves_kernel(own_ref, got_ref, keep_ref, send_ref):
@@ -356,7 +356,7 @@
         third = swap_z(features, 3)
         first = swap_z(features, 1)
         near = swap_x(features)
-        keep, send = pair_rows(near, features, first, third, second, ex_rows)
+        keep, send = pair_rows(near, features, third, first, second, ex_rows)
         keep, send = join_halves(keep, swap_across(send))
         return sum_rows(keep, swap_cores(send))
     share = ADAPTER_RANK * PROJ_ROWS // blocks

time: 21.4 us -> 21.9 us (1.023)
  starting transfers between devices: 8.4 us -> 8.73 us
    ppermute x3, waiting for transfers between devices: 3.9 us -> 4.42 us  [swap_z(): lax.ppermute(value, BLK + ('tensor',), [(i, i ^ other) for i in range(16)])]
    ppermute x1, starting transfers between devices: 0.92 us -> 1.24 us  [swap_across(): return lax.ppermute(value, ('x', 'tensor'), [(i, i ^ 3) for i in range(4)])]
    ppermute x1, waiting for transfers between devices: 2.14 us -> 1.81 us  [swap_across(): return lax.ppermute(value, ('x', 'tensor'), [(i, i ^ 3) for i in range(4)])]
where the time goes in v5:
time: 21.9 us; the launch traced here: 21.8 us
  starting transfers between devices  8.73 us (40%)
  waiting for transfers between devices  7.49 us (34%)
  Pallas kernels  5.55 us (25%)
    ppermute x3, starting transfers between devices, swap_z(): lax.ppermute(value, BLK + ('tensor',), [(i, i ^ other) for i in range(16)])  5.35 us
    ppermute x3, waiting for transfers between devices, swap_z(): lax.ppermute(value, BLK + ('tensor',), [(i, i ^ other) for i in range(16)])  4.42 us
    pallas_call x1, Pallas kernels, far_rows(): pl.pallas_call(functools.partial(far_kernel, cross, ex_rows), out_shape=[...  3.05 us
    ppermute x1, waiting for transfers between devices, swap_across(): return lax.ppermute(value, ('x', 'tensor'), [(i, i ^ 3) for i in range(4)])  1.81 us
    ppermute x1, starting transfers between devices, swap_x(): return lax.ppermute(value, 'x', [(0, 1), (1, 0)])  1.5 us
    ppermute x2, waiting for transfers between devices, swap_cores(): return lax.ppermute(value, 'tensor', [(0, 1), (1, 0)])  1.25 us
    ppermute x1, starting transfers between devices, swap_across(): return lax.ppermute(value, ('x', 'tensor'), [(i, i ^ 3) for i in range(4)])  1.24 us
    pallas_call x1, Pallas kernels, near_rows(): pl.pallas_call(near_kernel, out_shape=jax.ShapeDtypeStruct((PROJ_ROWS, to...  1.02 us
  transfers between devices with their start and end apart: 7, of which 5 were waited for; matrix products, arithmetic and copies ran while one was open for 0% of the time, Pallas kernels for 5%

profile of v5, /device:TPU:0, one launch (start us, length us, event | category | flops | bytes accessed | tf_op | source)
XLA Modules:
  0.0 21.8 jit_solution(3682126019113588324)
XLA Ops:
  0.0 3.0 %shard_map.64 = (bf16[304,512]{1,0:T(8,128)(2,1)S(1)}, bf16[48,512]{1,0:T(8,128)(2,1)S(1)}, bf16[512,2048]{1,0:T(8,128)(2,1)S(1)}, s32[16,256]{1,0:T(8,128)S(1)}...) custom-call(s32[4]{0:T(128)} %salts_hbm.1, s32[8,64]{1,0:T(8,128)} %mask_hbm.1, bf16[16,2048]{1,0:T(8,128)(2,1)} %down_hbm.1, ...), custom_call_target="tpu_custom_call" | custom-call | tf_op jit(solution)/shard_map/pallas_call | solution.py:170
  3.1 0.5 %collective-permute-start = (bf16[304,512]{1,0:T(8,128)(2,1)S(1)}, bf16[304,512]{1,0:T(8,128)(2,1)S(1)}, u32[]{:S(2)}, u32[]{:S(2)}) collective-permute-start(bf16[304,512]{1,0:T(8,128)(2,1)S(1)} %get-tuple-element.20), channel_id=1, source_target_pairs={{0,1},{1,0},{2,3},{3,2},{4,5},{5,4},{6,7},{7,6},{8,9},{9,8},{10,11... | collective-permute-start | bytes 933896 | tf_op jit(solution)/shard_map/ppermute | solution.py:320
  3.6 1.0 %shard_map.65.own_ref = bf16[256,512]{1,0:T(8,128)(2,1)S(1)} custom-call(s32[16,256]{1,0:T(8,128)S(1)} %get-tuple-element.17.start_ref, f32[8,512]{1,0:T(8,128)S(1)} %get-tuple-element.18.kept_ref, bf16[512,2048]{1,0:T(8,128)(2,1)S(1)} %get-tuple-element.19.near_ref), custom_call_target="tpu_custom_call" | custom-call | flops 536870912 | bytes 2097152 | tf_op jit(solution)/shard_map/pallas_call | solution.py:209
  4.6 0.2 collective-permute-done.other_ref
  4.8 0.4 %shard_map.66.own_ref = bf16[128,256]{1,0:T(8,128)(2,1)S(1)} custom-call(bf16[128,96]{1,0:T(8,128)(2,1)S(1)} %get-tuple-element.15.mixer_ref, bf16[48,512]{1,0:T(8,128)(2,1)S(1)} %get-tuple-element.16.ranks_ref, bf16[256,512]{1,0:T(8,128)(2,1)S(1)} %shard_map.65.own_ref, bf16[304,512]{1,0:T(8,128)(2,1)S(1)} %collective-permute-done.other_ref), custom_call_target="tpu_custom_call" | custom-call | tf_op jit(solution)/shard_map/pallas_call | solution.py:234
  5.2 3.8 %collective-permute-start.4 = (bf16[128,256]{1,0:T(8,128)(2,1)S(1)}, bf16[128,256]{1,0:T(8,128)(2,1)S(1)}, u32[]{:S(2)}, u32[]{:S(2)}) collective-permute-start(bf16[128,256]{1,0:T(8,128)(2,1)S(1)} %shard_map.66.own_ref), channel_id=1, source_target_pairs={{0,9},{1,8},{2,11},{3,10},{4,13},{5,12},{6,15},{7,14},{8,1},{9,0},... | collective-permute-start | bytes 196616 | tf_op jit(solution)/shard_map/ppermute | solution.py:333
  8.9 1.6 %collective-permute-start.3 = (bf16[128,256]{1,0:T(8,128)(2,1)S(1)}, bf16[128,256]{1,0:T(8,128)(2,1)S(1)}, u32[]{:S(2)}, u32[]{:S(2)}) collective-permute-start(bf16[128,256]{1,0:T(8,128)(2,1)S(1)} %shard_map.66.own_ref), channel_id=1, source_target_pairs={{0,4},{1,5},{2,6},{3,7},{4,0},{5,1},{6,2},{7,3},{8,12},{9,13},{10,... | collective-permute-start | bytes 196616 | tf_op jit(solution)/shard_map/ppermute | solution.py:333
  10.5 0.0 collective-permute-start.2
  10.5 1.5 %collective-permute-start.1 = (bf16[128,256]{1,0:T(8,128)(2,1)S(1)}, bf16[128,256]{1,0:T(8,128)(2,1)S(1)}, u32[]{:S(2)}, u32[]{:S(2)}) collective-permute-start(bf16[128,256]{1,0:T(8,128)(2,1)S(1)} %shard_map.66.own_ref), channel_id=1, source_target_pairs={{0,2},{2,0},{1,3},{3,1},{4,6},{6,4},{5,7},{7,5},{8,10},{10,8},{9,1... | collective-permute-start | bytes 196616 | tf_op jit(solution)/shard_map/ppermute | solution.py:328
  12.0 0.0 collective-permute-done.4.second_ref
  12.0 1.3 %collective-permute-done.3.first_ref = bf16[128,256]{1,0:T(8,128)(2,1)S(1)} collective-permute-done((bf16[128,256]{1,0:T(8,128)(2,1)S(1)}, bf16[128,256]{1,0:T(8,128)(2,1)S(1)}, u32[]{:S(2)}, u32[]{:S(2)}) %collective-permute-start.3) | collective-permute-done | bytes 65568 | tf_op jit(solution)/shard_map/ppermute | solution.py:333
  13.3 3.1 %collective-permute-done.2.third_ref = bf16[128,256]{1,0:T(8,128)(2,1)S(1)} collective-permute-done((bf16[128,256]{1,0:T(8,128)(2,1)S(1)}, bf16[128,256]{1,0:T(8,128)(2,1)S(1)}, u32[]{:S(2)}, u32[]{:S(2)}) %collective-permute-start.2) | collective-permute-done | bytes 65568 | tf_op jit(solution)/shard_map/ppermute | solution.py:333
  16.5 0.0 collective-permute-done.1.near_ref
  16.5 0.5 %shard_map.67 = (f32[8,128]{1,0:T(8,128)S(1)}, f32[8,128]{1,0:T(8,128)S(1)}) custom-call(bf16[128,256]{1,0:T(8,128)(2,1)S(1)} %collective-permute-done.1.near_ref, bf16[128,256]{1,0:T(8,128)(2,1)S(1)} %shard_map.66.own_ref, bf16[128,256]{1,0:T(8,128)(2,1)S(1)} %collective-permute-done.2.third_ref, bf16[128,256]{1,0:T(8,128)(2,1)S(1)} %collective-permute-done.3.first_ref, ...), custom_call_target="tpu_custom_call" | custom-call | tf_op jit(solution)/shard_map/pallas_call | solution.py:273
  16.9 1.2 %collective-permute-start.5 = (f32[8,128]{1,0:T(8,128)S(1)}, f32[8,128]{1,0:T(8,128)S(1)}, u32[]{:S(2)}, u32[]{:S(2)}) collective-permute-start(f32[8,128]{1,0:T(8,128)S(1)} %get-tuple-element.22), channel_id=1, source_target_pairs={{0,3},{1,2},{2,1},{3,0},{4,7},{5,6},{6,5},{7,4},{8,11},{9,10},{10,... | collective-permute-start | bytes 12296 | tf_op jit(solution)/shard_map/ppermute | solution.py:324
  18.2 1.8 %collective-permute-done.5.got_ref = f32[8,128]{1,0:T(8,128)S(1)} collective-permute-done((f32[8,128]{1,0:T(8,128)S(1)}, f32[8,128]{1,0:T(8,128)S(1)}, u32[]{:S(2)}, u32[]{:S(2)}) %collective-permute-start.5) | collective-permute-done | bytes 4128 | tf_op jit(solution)/shard_map/ppermute | solution.py:324
  20.0 0.1 shard_map.68
  20.1 0.1 collective-permute-start.6
  20.2 1.0 %collective-permute-done.6.got_ref = f32[4,128]{1,0:T(4,128)S(1)} collective-permute-done((f32[4,128]{1,0:T(4,128)S(1)}, f32[4,128]{1,0:T(4,128)S(1)}, u32[]{:S(2)}, u32[]{:S(2)}) %collective-permute-start.6) | collective-permute-done | bytes 2080 | tf_op jit(solution)/shard_map/ppermute | solution.py:320
  21.2 0.6 %shard_map.69 = f32[4,64]{1,0:T(4,128)} custom-call(f32[4,128]{1,0:T(4,128)S(1)} %get-tuple-element.23.keep_ref, f32[4,128]{1,0:T(4,128)S(1)} %collective-permute-done.6.got_ref), custom_call_target="tpu_custom_call" | custom-call | tf_op jit(solution)/shard_map/pallas_call | solution.py:310
Async XLA Ops:
  3.1 1.7 %collective-permute-start = (bf16[304,512]{1,0:T(8,128)(2,1)S(1)}, bf16[304,512]{1,0:T(8,128)(2,1)S(1)}, u32[]{:S(2)}, u32[]{:S(2)}) collective-permute-start(bf16[304,512]{1,0:T(8,128)(2,1)S(1)} %get-tuple-element.20), channel_id=1, source_target_pairs={{0,1},{1,0},{2,3},{3,2},{4,5},{5,4},{6,7},{7,6},{8,9},{9,8},{10,11... | collective-permute-start | bytes 933896 | tf_op jit(solution)/shard_map/ppermute | solution.py:320
  5.2 6.9 %collective-permute-start.4 = (bf16[128,256]{1,0:T(8,128)(2,1)S(1)}, bf16[128,256]{1,0:T(8,128)(2,1)S(1)}, u32[]{:S(2)}, u32[]{:S(2)}) collective-permute-start(bf16[128,256]{1,0:T(8,128)(2,1)S(1)} %shard_map.66.own_ref), channel_id=1, source_target_pairs={{0,9},{1,8},{2,11},{3,10},{4,13},{5,12},{6,15},{7,14},{8,1},{9,0},... | collective-permute-start | bytes 196616 | tf_op jit(solution)/shard_map/ppermute | solution.py:333
  8.9 4.4 %collective-permute-start.3 = (bf16[128,256]{1,0:T(8,128)(2,1)S(1)}, bf16[128,256]{1,0:T(8,128)(2,1)S(1)}, u32[]{:S(2)}, u32[]{:S(2)}) collective-permute-start(bf16[128,256]{1,0:T(8,128)(2,1)S(1)} %shard_map.66.own_ref), channel_id=1, source_target_pairs={{0,4},{1,5},{2,6},{3,7},{4,0},{5,1},{6,2},{7,3},{8,12},{9,13},{10,... | collective-permute-start | bytes 196616 | tf_op jit(solution)/shard_map/ppermute | solution.py:333
  10.5 5.9 %collective-permute-start.2 = (bf16[128,256]{1,0:T(8,128)(2,1)S(1)}, bf16[128,256]{1,0:T(8,128)(2,1)S(1)}, u32[]{:S(2)}, u32[]{:S(2)}) collective-permute-start(bf16[128,256]{1,0:T(8,128)(2,1)S(1)} %shard_map.66.own_ref), channel_id=1, source_target_pairs={{0,13},{1,12},{2,15},{3,14},{4,9},{5,8},{6,11},{7,10},{8,5},{9,4},... | collective-permute-start | bytes 196616 | tf_op jit(solution)/shard_map/ppermute | solution.py:333
  10.5 5.9 %collective-permute-start.1 = (bf16[128,256]{1,0:T(8,128)(2,1)S(1)}, bf16[128,256]{1,0:T(8,128)(2,1)S(1)}, u32[]{:S(2)}, u32[]{:S(2)}) collective-permute-start(bf16[128,256]{1,0:T(8,128)(2,1)S(1)} %shard_map.66.own_ref), channel_id=1, source_target_pairs={{0,2},{2,0},{1,3},{3,1},{4,6},{6,4},{5,7},{7,5},{8,10},{10,8},{9,1... | collective-permute-start | bytes 196616 | tf_op jit(solution)/shard_map/ppermute | solution.py:328
  16.9 3.1 %collective-permute-start.5 = (f32[8,128]{1,0:T(8,128)S(1)}, f32[8,128]{1,0:T(8,128)S(1)}, u32[]{:S(2)}, u32[]{:S(2)}) collective-permute-start(f32[8,128]{1,0:T(8,128)S(1)} %get-tuple-element.22), channel_id=1, source_target_pairs={{0,3},{1,2},{2,1},{3,0},{4,7},{5,6},{6,5},{7,4},{8,11},{9,10},{10,... | collective-permute-start | bytes 12296 | tf_op jit(solution)/shard_map/ppermute | solution.py:324
  20.1 1.2 %collective-permute-start.6 = (f32[4,128]{1,0:T(4,128)S(1)}, f32[4,128]{1,0:T(4,128)S(1)}, u32[]{:S(2)}, u32[]{:S(2)}) collective-permute-start(f32[4,128]{1,0:T(4,128)S(1)} %get-tuple-element.24), channel_id=1, source_target_pairs={{0,1},{1,0},{2,3},{3,2},{4,5},{5,4},{6,7},{7,6},{8,9},{9,8},{10,11... | collective-permute-start | bytes 6152 | tf_op jit(solution)/shard_map/ppermute | solution.py:320

commit v6 on v5

--- a/solution.py
+++ b/solution.py
@@ -254,14 +254,18 @@
     return jnp.where((z & 1) != 0, swapped, rows)
 
 
-def pair_kernel(ex_rows, near_ref, own_ref, third_ref, first_ref, second_ref, keep_ref, send_ref):
-    z_refs = (own_ref, first_ref, second_ref, third_ref)
+def pair_kernel(ex_rows, near_ref, own_ref, third_got_ref, second_got_ref, first_got_ref, *out_refs):
+    keep_ref, send_ref = out_refs
+    z = lax.axis_index("z")
+    inner = (z == 1) | (z == 2)
     wide = 2 * ex_rows
     total = None
-    for row in range(0, near_ref.shape[0], wide):
+    for row in range(0, own_ref.shape[0], wide):
         part = slice(row, row + wide)
-        left = jnp.concatenate([z_refs[0][part, :], near_ref[part, :]], axis=0)
-        right = jnp.concatenate([ref[part, :] for ref in z_refs], axis=0)
+        own, one, two = own_ref[part, :], first_got_ref[part, :], third_got_ref[part, :]
+        left = jnp.concatenate([own, near_ref[part, :]], axis=0)
+        by_z = [own, jnp.where(inner, one, two), jnp.where(inner, two, one)]
+        right = jnp.concatenate(by_z + [second_got_ref[part, :]], axis=0)
         term = lax.dot_general(left, right, NT, preferred_element_type=F32)
         total = term if total is None else total + term
     total = jnp.concatenate([total, total], axis=1)
@@ -269,14 +273,14 @@
     send_ref[...] = order_blocks(fold_ranks(total[wide:]), wide)
 
 
-def pair_rows(near, own, third, first, second, ex_rows):
+def pair_rows(near, own, third, second, first, ex_rows):
     return pl.pallas_call(
         functools.partial(pair_kernel, ex_rows),
         out_shape=[jax.ShapeDtypeStruct((ex_rows, LANES), F32)] * 2,
         in_specs=[VMEM] * 5,
         out_specs=[VMEM] * 2,
         compiler_params=SMALL,
-    )(near, own, third, first, second)
+    )(near, own, third, second, first)
 
 
 def halves_kernel(own_ref, got_ref, keep_ref, send_ref):
@@ -328,9 +332,13 @@
     return lax.ppermute(value, "x", [(0, 1), (1, 0)])
 
 
-def swap_z(value, step):
-    other = 4 * step + (step > 1)
-    return lax.ppermute(value, BLK + ("tensor",), [(i, i ^ other) for i in range(16)])
+def step_z(value, targets):
+    pairs = []
+    for z, target in enumerate(targets):
+        for x in range(2):
+            for kind in range(2):
+                pairs.append(tuple(4 * at + 2 * x + (kind ^ (at // 2)) for at in (z, target)))
+    return lax.ppermute(value, BLK + ("tensor",), pairs)
 
 
 def body(
@@ -352,11 +360,11 @@
     terms = (mixer, ranks, near_rows(start, kept, near), other)
     features = feature_rows(*terms, ex_rows)
     if fast:
-        second = swap_z(features, 2)
-        third = swap_z(features, 3)
-        first = swap_z(features, 1)
+        first = step_z(features, (1, 3, 0, 2))
+        second = step_z(features, (3, 2, 1, 0))
+        third = step_z(features, (2, 0, 3, 1))
         near = swap_x(features)
-        keep, send = pair_rows(near, features, third, first, second, ex_rows)
+        keep, send = pair_rows(near, features, third, second, first, ex_rows)
         keep, send = join_halves(keep, swap_across(send))
         return sum_rows(keep, swap_cores(send))
     share = ADAPTER_RANK * PROJ_ROWS // blocks

time: 21.9 us -> 21.6 us (0.986)
  waiting for transfers between devices: 7.49 us -> 6.12 us
  starting transfers between devices: 8.73 us -> 9.7 us
    ppermute x3, waiting for transfers between devices: 4.42 us -> 2.66 us  [step_z(): return lax.ppermute(value, BLK + ('tensor',), pairs)]
    ppermute x3, starting transfers between devices: 5.35 us -> 6.53 us  [step_z(): return lax.ppermute(value, BLK + ('tensor',), pairs)]
  transfers between devices with their start and end apart: 7 -> 7, of which waited for: 5 -> 6; matrix products, arithmetic and copies ran while one was open for 0% -> 0% of each run, Pallas kernels for 5% -> 5%
where the time goes in v6:
time: 21.6 us; the launch traced here: 21.4 us
  starting transfers between devices  9.7 us (45%)
  waiting for transfers between devices  6.12 us (28%)
  Pallas kernels  5.55 us (26%)
    ppermute x3, starting transfers between devices, step_z(): return lax.ppermute(value, BLK + ('tensor',), pairs)  6.53 us
    pallas_call x1, Pallas kernels, far_rows(): pl.pallas_call(functools.partial(far_kernel, cross, ex_rows), out_shape=[...  3.05 us
    ppermute x3, waiting for transfers between devices, step_z(): return lax.ppermute(value, BLK + ('tensor',), pairs)  2.66 us
    ppermute x1, waiting for transfers between devices, swap_across(): return lax.ppermute(value, ('x', 'tensor'), [(i, i ^ 3) for i in range(4)])  2.03 us
    ppermute x1, starting transfers between devices, swap_x(): return lax.ppermute(value, 'x', [(0, 1), (1, 0)])  1.52 us
    ppermute x2, waiting for transfers between devices, swap_cores(): return lax.ppermute(value, 'tensor', [(0, 1), (1, 0)])  1.25 us
    ppermute x1, starting transfers between devices, swap_across(): return lax.ppermute(value, ('x', 'tensor'), [(i, i ^ 3) for i in range(4)])  1.02 us
    pallas_call x1, Pallas kernels, near_rows(): pl.pallas_call(near_kernel, out_shape=jax.ShapeDtypeStruct((PROJ_ROWS, to...  1.02 us
  transfers between devices with their start and end apart: 7, of which 6 were waited for; matrix products, arithmetic and copies ran while one was open for 0% of the time, Pallas kernels for 5%

profile of v6, /device:TPU:0, one launch (start us, length us, event | category | flops | bytes accessed | tf_op | source)
XLA Modules:
  0.0 21.4 jit_solution(15906618270709349469)
XLA Ops:
  0.0 3.0 %shard_map.64 = (bf16[304,512]{1,0:T(8,128)(2,1)S(1)}, bf16[48,512]{1,0:T(8,128)(2,1)S(1)}, bf16[512,2048]{1,0:T(8,128)(2,1)S(1)}, s32[16,256]{1,0:T(8,128)S(1)}...) custom-call(s32[4]{0:T(128)} %salts_hbm.1, s32[8,64]{1,0:T(8,128)} %mask_hbm.1, bf16[16,2048]{1,0:T(8,128)(2,1)} %down_hbm.1, ...), custom_call_target="tpu_custom_call" | custom-call | tf_op jit(solution)/shard_map/pallas_call | solution.py:170
  3.1 0.5 %collective-permute-start = (bf16[304,512]{1,0:T(8,128)(2,1)S(1)}, bf16[304,512]{1,0:T(8,128)(2,1)S(1)}, u32[]{:S(2)}, u32[]{:S(2)}) collective-permute-start(bf16[304,512]{1,0:T(8,128)(2,1)S(1)} %get-tuple-element.20), channel_id=1, source_target_pairs={{0,1},{1,0},{2,3},{3,2},{4,5},{5,4},{6,7},{7,6},{8,9},{9,8},{10,11... | collective-permute-start | bytes 933896 | tf_op jit(solution)/shard_map/ppermute | solution.py:324
  3.6 1.0 %shard_map.65.own_ref = bf16[256,512]{1,0:T(8,128)(2,1)S(1)} custom-call(s32[16,256]{1,0:T(8,128)S(1)} %get-tuple-element.17.start_ref, f32[8,512]{1,0:T(8,128)S(1)} %get-tuple-element.18.kept_ref, bf16[512,2048]{1,0:T(8,128)(2,1)S(1)} %get-tuple-element.19.near_ref), custom_call_target="tpu_custom_call" | custom-call | flops 536870912 | bytes 2097152 | tf_op jit(solution)/shard_map/pallas_call | solution.py:209
  4.6 0.2 collective-permute-done.other_ref
  4.8 0.4 %shard_map.66.own_ref = bf16[128,256]{1,0:T(8,128)(2,1)S(1)} custom-call(bf16[128,96]{1,0:T(8,128)(2,1)S(1)} %get-tuple-element.15.mixer_ref, bf16[48,512]{1,0:T(8,128)(2,1)S(1)} %get-tuple-element.16.ranks_ref, bf16[256,512]{1,0:T(8,128)(2,1)S(1)} %shard_map.65.own_ref, bf16[304,512]{1,0:T(8,128)(2,1)S(1)} %collective-permute-done.other_ref), custom_call_target="tpu_custom_call" | custom-call | tf_op jit(solution)/shard_map/pallas_call | solution.py:234
  5.2 3.0 %collective-permute-start.4 = (bf16[128,256]{1,0:T(8,128)(2,1)S(1)}, bf16[128,256]{1,0:T(8,128)(2,1)S(1)}, u32[]{:S(2)}, u32[]{:S(2)}) collective-permute-start(bf16[128,256]{1,0:T(8,128)(2,1)S(1)} %shard_map.66.own_ref), channel_id=1, source_target_pairs={{0,4},{1,5},{2,6},{3,7},{4,13},{5,12},{6,15},{7,14},{9,0},{8,1},{1... | collective-permute-start | bytes 196616 | tf_op jit(solution)/shard_map/ppermute | solution.py:341
  8.2 1.9 %collective-permute-start.3 = (bf16[128,256]{1,0:T(8,128)(2,1)S(1)}, bf16[128,256]{1,0:T(8,128)(2,1)S(1)}, u32[]{:S(2)}, u32[]{:S(2)}) collective-permute-start(bf16[128,256]{1,0:T(8,128)(2,1)S(1)} %shard_map.66.own_ref), channel_id=1, source_target_pairs={{0,13},{1,12},{2,15},{3,14},{4,9},{5,8},{6,11},{7,10},{9,4},{8,5},... | collective-permute-start | bytes 196616 | tf_op jit(solution)/shard_map/ppermute | solution.py:341
  10.1 1.6 %collective-permute-start.2 = (bf16[128,256]{1,0:T(8,128)(2,1)S(1)}, bf16[128,256]{1,0:T(8,128)(2,1)S(1)}, u32[]{:S(2)}, u32[]{:S(2)}) collective-permute-start(bf16[128,256]{1,0:T(8,128)(2,1)S(1)} %shard_map.66.own_ref), channel_id=1, source_target_pairs={{0,9},{1,8},{2,11},{3,10},{4,0},{5,1},{6,2},{7,3},{9,13},{8,12},{1... | collective-permute-start | bytes 196616 | tf_op jit(solution)/shard_map/ppermute | solution.py:341
  11.7 1.5 %collective-permute-start.1 = (bf16[128,256]{1,0:T(8,128)(2,1)S(1)}, bf16[128,256]{1,0:T(8,128)(2,1)S(1)}, u32[]{:S(2)}, u32[]{:S(2)}) collective-permute-start(bf16[128,256]{1,0:T(8,128)(2,1)S(1)} %shard_map.66.own_ref), channel_id=1, source_target_pairs={{0,2},{2,0},{1,3},{3,1},{4,6},{6,4},{5,7},{7,5},{8,10},{10,8},{9,1... | collective-permute-start | bytes 196616 | tf_op jit(solution)/shard_map/ppermute | solution.py:332
  13.2 0.0 collective-permute-done.4.first_got_ref
  13.2 1.3 %collective-permute-done.3.second_got_ref = bf16[128,256]{1,0:T(8,128)(2,1)S(1)} collective-permute-done((bf16[128,256]{1,0:T(8,128)(2,1)S(1)}, bf16[128,256]{1,0:T(8,128)(2,1)S(1)}, u32[]{:S(2)}, u32[]{:S(2)}) %collective-permute-start.3) | collective-permute-done | bytes 65568 | tf_op jit(solution)/shard_map/ppermute | solution.py:341
  14.6 1.3 %collective-permute-done.2.third_got_ref = bf16[128,256]{1,0:T(8,128)(2,1)S(1)} collective-permute-done((bf16[128,256]{1,0:T(8,128)(2,1)S(1)}, bf16[128,256]{1,0:T(8,128)(2,1)S(1)}, u32[]{:S(2)}, u32[]{:S(2)}) %collective-permute-start.2) | collective-permute-done | bytes 65568 | tf_op jit(solution)/shard_map/ppermute | solution.py:341
  15.9 0.2 collective-permute-done.1.near_ref
  16.1 0.5 %shard_map.67 = (f32[8,128]{1,0:T(8,128)S(1)}, f32[8,128]{1,0:T(8,128)S(1)}) custom-call(bf16[128,256]{1,0:T(8,128)(2,1)S(1)} %collective-permute-done.1.near_ref, bf16[128,256]{1,0:T(8,128)(2,1)S(1)} %shard_map.66.own_ref, bf16[128,256]{1,0:T(8,128)(2,1)S(1)} %collective-permute-done.2.third_got_ref, ...), custom_call_target="tpu_custom_call" | custom-call | tf_op jit(solution)/shard_map/pallas_call | solution.py:277
  16.5 1.0 %collective-permute-start.5 = (f32[8,128]{1,0:T(8,128)S(1)}, f32[8,128]{1,0:T(8,128)S(1)}, u32[]{:S(2)}, u32[]{:S(2)}) collective-permute-start(f32[8,128]{1,0:T(8,128)S(1)} %get-tuple-element.22), channel_id=1, source_target_pairs={{0,3},{1,2},{2,1},{3,0},{4,7},{5,6},{6,5},{7,4},{8,11},{9,10},{10,... | collective-permute-start | bytes 12296 | tf_op jit(solution)/shard_map/ppermute | solution.py:328
  17.6 2.0 %collective-permute-done.5.got_ref = f32[8,128]{1,0:T(8,128)S(1)} collective-permute-done((f32[8,128]{1,0:T(8,128)S(1)}, f32[8,128]{1,0:T(8,128)S(1)}, u32[]{:S(2)}, u32[]{:S(2)}) %collective-permute-start.5) | collective-permute-done | bytes 4128 | tf_op jit(solution)/shard_map/ppermute | solution.py:328
  19.6 0.1 shard_map.68
  19.7 0.1 collective-permute-start.6
  19.8 1.0 %collective-permute-done.6.got_ref = f32[4,128]{1,0:T(4,128)S(1)} collective-permute-done((f32[4,128]{1,0:T(4,128)S(1)}, f32[4,128]{1,0:T(4,128)S(1)}, u32[]{:S(2)}, u32[]{:S(2)}) %collective-permute-start.6) | collective-permute-done | bytes 2080 | tf_op jit(solution)/shard_map/ppermute | solution.py:324
  20.8 0.6 %shard_map.69 = f32[4,64]{1,0:T(4,128)} custom-call(f32[4,128]{1,0:T(4,128)S(1)} %get-tuple-element.23.keep_ref, f32[4,128]{1,0:T(4,128)S(1)} %collective-permute-done.6.got_ref), custom_call_target="tpu_custom_call" | custom-call | tf_op jit(solution)/shard_map/pallas_call | solution.py:314
Async XLA Ops:
  3.1 1.7 %collective-permute-start = (bf16[304,512]{1,0:T(8,128)(2,1)S(1)}, bf16[304,512]{1,0:T(8,128)(2,1)S(1)}, u32[]{:S(2)}, u32[]{:S(2)}) collective-permute-start(bf16[304,512]{1,0:T(8,128)(2,1)S(1)} %get-tuple-element.20), channel_id=1, source_target_pairs={{0,1},{1,0},{2,3},{3,2},{4,5},{5,4},{6,7},{7,6},{8,9},{9,8},{10,11... | collective-permute-start | bytes 933896 | tf_op jit(solution)/shard_map/ppermute | solution.py:324
  5.2 8.1 %collective-permute-start.4 = (bf16[128,256]{1,0:T(8,128)(2,1)S(1)}, bf16[128,256]{1,0:T(8,128)(2,1)S(1)}, u32[]{:S(2)}, u32[]{:S(2)}) collective-permute-start(bf16[128,256]{1,0:T(8,128)(2,1)S(1)} %shard_map.66.own_ref), channel_id=1, source_target_pairs={{0,4},{1,5},{2,6},{3,7},{4,13},{5,12},{6,15},{7,14},{9,0},{8,1},{1... | collective-permute-start | bytes 196616 | tf_op jit(solution)/shard_map/ppermute | solution.py:341
  8.2 6.4 %collective-permute-start.3 = (bf16[128,256]{1,0:T(8,128)(2,1)S(1)}, bf16[128,256]{1,0:T(8,128)(2,1)S(1)}, u32[]{:S(2)}, u32[]{:S(2)}) collective-permute-start(bf16[128,256]{1,0:T(8,128)(2,1)S(1)} %shard_map.66.own_ref), channel_id=1, source_target_pairs={{0,13},{1,12},{2,15},{3,14},{4,9},{5,8},{6,11},{7,10},{9,4},{8,5},... | collective-permute-start | bytes 196616 | tf_op jit(solution)/shard_map/ppermute | solution.py:341
  10.1 5.8 %collective-permute-start.2 = (bf16[128,256]{1,0:T(8,128)(2,1)S(1)}, bf16[128,256]{1,0:T(8,128)(2,1)S(1)}, u32[]{:S(2)}, u32[]{:S(2)}) collective-permute-start(bf16[128,256]{1,0:T(8,128)(2,1)S(1)} %shard_map.66.own_ref), channel_id=1, source_target_pairs={{0,9},{1,8},{2,11},{3,10},{4,0},{5,1},{6,2},{7,3},{9,13},{8,12},{1... | collective-permute-start | bytes 196616 | tf_op jit(solution)/shard_map/ppermute | solution.py:341
  11.7 4.4 %collective-permute-start.1 = (bf16[128,256]{1,0:T(8,128)(2,1)S(1)}, bf16[128,256]{1,0:T(8,128)(2,1)S(1)}, u32[]{:S(2)}, u32[]{:S(2)}) collective-permute-start(bf16[128,256]{1,0:T(8,128)(2,1)S(1)} %shard_map.66.own_ref), channel_id=1, source_target_pairs={{0,2},{2,0},{1,3},{3,1},{4,6},{6,4},{5,7},{7,5},{8,10},{10,8},{9,1... | collective-permute-start | bytes 196616 | tf_op jit(solution)/shard_map/ppermute | solution.py:332
  16.5 3.1 %collective-permute-start.5 = (f32[8,128]{1,0:T(8,128)S(1)}, f32[8,128]{1,0:T(8,128)S(1)}, u32[]{:S(2)}, u32[]{:S(2)}) collective-permute-start(f32[8,128]{1,0:T(8,128)S(1)} %get-tuple-element.22), channel_id=1, source_target_pairs={{0,3},{1,2},{2,1},{3,0},{4,7},{5,6},{6,5},{7,4},{8,11},{9,10},{10,... | collective-permute-start | bytes 12296 | tf_op jit(solution)/shard_map/ppermute | solution.py:328
  19.7 1.2 %collective-permute-start.6 = (f32[4,128]{1,0:T(4,128)S(1)}, f32[4,128]{1,0:T(4,128)S(1)}, u32[]{:S(2)}, u32[]{:S(2)}) collective-permute-start(f32[4,128]{1,0:T(4,128)S(1)} %get-tuple-element.24), channel_id=1, source_target_pairs={{0,1},{1,0},{2,3},{3,2},{4,5},{5,4},{6,7},{7,6},{8,9},{9,8},{10,11... | collective-permute-start | bytes 6152 | tf_op jit(solution)/shard_map/ppermute | solution.py:324

commit v7 on v3

--- a/solution.py
+++ b/solution.py
@@ -16,6 +16,7 @@
 PIECES = 3
 LANES = 128
 BLOCK = (16, 256)
+LEAD = 3
 BLK = ("z", "x")
 
 F32 = jnp.float32
@@ -141,12 +142,15 @@
     far_kept = counted | (kind == 0)
     near_kept = counted | (kind == 1)
     kept_ref[...] = jnp.broadcast_to(jnp.where(near_kept, 1.0, 0.0), kept_ref.shape)
+    ahead = [sign_rows(far_start, col) for col in range(0, LEAD * wide, wide)]
     far_waits[0].wait()
     near_waits[0].wait()
     total = ranks = None
     for col in range(0, width, wide):
         part = slice(col, col + wide)
-        left = jnp.concatenate(sign_rows(far_start, col) + [far_factor[:, part]], axis=0)
+        if col + LEAD * wide < width:
+            ahead.append(sign_rows(far_start, col + LEAD * wide))
+        left = jnp.concatenate(ahead.pop(0) + [far_factor[:, part]], axis=0)
         if col in ends:
             far_waits[1 + ends.index(col)].wait()
             near_waits[1 + ends.index(col)].wait()

time: 21.4 us -> 21.4 us (level)
  no operation moved by 1% of the time
where the time goes in v7:
time: 21.4 us; the launch traced here: 21.2 us
  starting transfers between devices  8.95 us (42%)
  waiting for transfers between devices  6.72 us (31%)
  Pallas kernels  5.53 us (26%)
    ppermute x3, starting transfers between devices, swap_z(): lax.ppermute(value, BLK + ('tensor',), [(i, i ^ other) for i in range(16)])  5.43 us
    ppermute x3, waiting for transfers between devices, swap_z(): lax.ppermute(value, BLK + ('tensor',), [(i, i ^ other) for i in range(16)])  3.69 us
    pallas_call x1, Pallas kernels, far_rows(): pl.pallas_call(functools.partial(far_kernel, cross, ex_rows), out_shape=[...  3.02 us
    ppermute x1, waiting for transfers between devices, swap_across(): return lax.ppermute(value, ('x', 'tensor'), [(i, i ^ 3) for i in range(4)])  1.79 us
    ppermute x1, starting transfers between devices, swap_x(): return lax.ppermute(value, 'x', [(0, 1), (1, 0)])  1.6 us
    ppermute x1, starting transfers between devices, swap_across(): return lax.ppermute(value, ('x', 'tensor'), [(i, i ^ 3) for i in range(4)])  1.26 us
    ppermute x2, waiting for transfers between devices, swap_cores(): return lax.ppermute(value, 'tensor', [(0, 1), (1, 0)])  1.23 us
    pallas_call x1, Pallas kernels, near_rows(): pl.pallas_call(near_kernel, out_shape=jax.ShapeDtypeStruct((PROJ_ROWS, to...  1.02 us
  transfers between devices with their start and end apart: 7, of which 5 were waited for; matrix products, arithmetic and copies ran while one was open for 0% of the time, Pallas kernels for 5%

profile of v7, /device:TPU:0, one launch (start us, length us, event | category | flops | bytes accessed | tf_op | source)
XLA Modules:
  0.0 21.2 jit_solution(14111443351945544622)
XLA Ops:
  0.0 3.0 %shard_map.64 = (bf16[304,512]{1,0:T(8,128)(2,1)S(1)}, bf16[48,512]{1,0:T(8,128)(2,1)S(1)}, bf16[512,2048]{1,0:T(8,128)(2,1)S(1)}, s32[16,256]{1,0:T(8,128)S(1)}...) custom-call(s32[4]{0:T(128)} %salts_hbm.1, s32[8,64]{1,0:T(8,128)} %mask_hbm.1, bf16[16,2048]{1,0:T(8,128)(2,1)} %down_hbm.1, ...), custom_call_target="tpu_custom_call" | custom-call | tf_op jit(solution)/shard_map/pallas_call | solution.py:174
  3.0 0.5 %collective-permute-start = (bf16[304,512]{1,0:T(8,128)(2,1)S(1)}, bf16[304,512]{1,0:T(8,128)(2,1)S(1)}, u32[]{:S(2)}, u32[]{:S(2)}) collective-permute-start(bf16[304,512]{1,0:T(8,128)(2,1)S(1)} %get-tuple-element.20), channel_id=1, source_target_pairs={{0,1},{1,0},{2,3},{3,2},{4,5},{5,4},{6,7},{7,6},{8,9},{9,8},{10,11... | collective-permute-start | bytes 933896 | tf_op jit(solution)/shard_map/ppermute | solution.py:324
  3.5 1.0 %shard_map.65.own_ref = bf16[256,512]{1,0:T(8,128)(2,1)S(1)} custom-call(s32[16,256]{1,0:T(8,128)S(1)} %get-tuple-element.17.start_ref, f32[8,512]{1,0:T(8,128)S(1)} %get-tuple-element.18.kept_ref, bf16[512,2048]{1,0:T(8,128)(2,1)S(1)} %get-tuple-element.19.near_ref), custom_call_target="tpu_custom_call" | custom-call | flops 536870912 | bytes 2097152 | tf_op jit(solution)/shard_map/pallas_call | solution.py:213
  4.6 0.2 %collective-permute-done.other_ref = bf16[304,512]{1,0:T(8,128)(2,1)S(1)} collective-permute-done((bf16[304,512]{1,0:T(8,128)(2,1)S(1)}, bf16[304,512]{1,0:T(8,128)(2,1)S(1)}, u32[]{:S(2)}, u32[]{:S(2)}) %collective-permute-start) | collective-permute-done | bytes 311328 | tf_op jit(solution)/shard_map/ppermute | solution.py:324
  4.8 0.4 %shard_map.66.refs_0_ = bf16[128,256]{1,0:T(8,128)(2,1)S(1)} custom-call(bf16[128,96]{1,0:T(8,128)(2,1)S(1)} %get-tuple-element.15.mixer_ref, bf16[48,512]{1,0:T(8,128)(2,1)S(1)} %get-tuple-element.16.ranks_ref, bf16[256,512]{1,0:T(8,128)(2,1)S(1)} %shard_map.65.own_ref, bf16[304,512]{1,0:T(8,128)(2,1)S(1)} %collective-permute-done.other_ref), custom_call_target="tpu_custom_call" | custom-call | tf_op jit(solution)/shard_map/pallas_call | solution.py:238
  5.2 4.8 %collective-permute-start.4 = (bf16[128,256]{1,0:T(8,128)(2,1)S(1)}, bf16[128,256]{1,0:T(8,128)(2,1)S(1)}, u32[]{:S(2)}, u32[]{:S(2)}) collective-permute-start(bf16[128,256]{1,0:T(8,128)(2,1)S(1)} %shard_map.66.refs_0_), channel_id=1, source_target_pairs={{0,13},{1,12},{2,15},{3,14},{4,9},{5,8},{6,11},{7,10},{8,5},{9,4},... | collective-permute-start | bytes 196616 | tf_op jit(solution)/shard_map/ppermute | solution.py:337
  9.9 0.0 collective-permute-start.3
  9.9 0.7 %collective-permute-start.2 = (bf16[128,256]{1,0:T(8,128)(2,1)S(1)}, bf16[128,256]{1,0:T(8,128)(2,1)S(1)}, u32[]{:S(2)}, u32[]{:S(2)}) collective-permute-start(bf16[128,256]{1,0:T(8,128)(2,1)S(1)} %shard_map.66.refs_0_), channel_id=1, source_target_pairs={{0,4},{1,5},{2,6},{3,7},{4,0},{5,1},{6,2},{7,3},{8,12},{9,13},{10,... | collective-permute-start | bytes 196616 | tf_op jit(solution)/shard_map/ppermute | solution.py:337
  10.6 1.6 %collective-permute-start.1 = (bf16[128,256]{1,0:T(8,128)(2,1)S(1)}, bf16[128,256]{1,0:T(8,128)(2,1)S(1)}, u32[]{:S(2)}, u32[]{:S(2)}) collective-permute-start(bf16[128,256]{1,0:T(8,128)(2,1)S(1)} %shard_map.66.refs_0_), channel_id=1, source_target_pairs={{0,2},{2,0},{1,3},{3,1},{4,6},{6,4},{5,7},{7,5},{8,10},{10,8},{9,1... | collective-permute-start | bytes 196616 | tf_op jit(solution)/shard_map/ppermute | solution.py:332
  12.2 0.3 %collective-permute-done.4.refs_3_ = bf16[128,256]{1,0:T(8,128)(2,1)S(1)} collective-permute-done((bf16[128,256]{1,0:T(8,128)(2,1)S(1)}, bf16[128,256]{1,0:T(8,128)(2,1)S(1)}, u32[]{:S(2)}, u32[]{:S(2)}) %collective-permute-start.4) | collective-permute-done | bytes 65568 | tf_op jit(solution)/shard_map/ppermute | solution.py:337
  12.5 3.4 %collective-permute-done.3.refs_2_ = bf16[128,256]{1,0:T(8,128)(2,1)S(1)} collective-permute-done((bf16[128,256]{1,0:T(8,128)(2,1)S(1)}, bf16[128,256]{1,0:T(8,128)(2,1)S(1)}, u32[]{:S(2)}, u32[]{:S(2)}) %collective-permute-start.3) | collective-permute-done | bytes 65568 | tf_op jit(solution)/shard_map/ppermute | solution.py:337
  15.9 0.0 collective-permute-done.2.refs_1_
  15.9 0.0 collective-permute-done.1.near_ref
  15.9 0.5 %shard_map.67 = (f32[8,128]{1,0:T(8,128)S(1)}, f32[8,128]{1,0:T(8,128)S(1)}) custom-call(bf16[128,256]{1,0:T(8,128)(2,1)S(1)} %collective-permute-done.1.near_ref, bf16[128,256]{1,0:T(8,128)(2,1)S(1)} %shard_map.66.refs_0_, bf16[128,256]{1,0:T(8,128)(2,1)S(1)} %collective-permute-done.2.refs_1_, bf16[128,256]{1,0:T(8,128)(2,1)S(1)} %collective-permute-done.3.refs_2_, ...), custom_call_target="tpu_custom_call" | custom-call | tf_op jit(solution)/shard_map/pallas_call | solution.py:277
  16.4 1.3 %collective-permute-start.5 = (f32[8,128]{1,0:T(8,128)S(1)}, f32[8,128]{1,0:T(8,128)S(1)}, u32[]{:S(2)}, u32[]{:S(2)}) collective-permute-start(f32[8,128]{1,0:T(8,128)S(1)} %get-tuple-element.22), channel_id=1, source_target_pairs={{0,3},{1,2},{2,1},{3,0},{4,7},{5,6},{6,5},{7,4},{8,11},{9,10},{10,... | collective-permute-start | bytes 12296 | tf_op jit(solution)/shard_map/ppermute | solution.py:328
  17.6 1.8 %collective-permute-done.5.got_ref = f32[8,128]{1,0:T(8,128)S(1)} collective-permute-done((f32[8,128]{1,0:T(8,128)S(1)}, f32[8,128]{1,0:T(8,128)S(1)}, u32[]{:S(2)}, u32[]{:S(2)}) %collective-permute-start.5) | collective-permute-done | bytes 4128 | tf_op jit(solution)/shard_map/ppermute | solution.py:328
  19.4 0.1 shard_map.68
  19.5 0.1 collective-permute-start.6
  19.6 1.0 %collective-permute-done.6.got_ref = f32[4,128]{1,0:T(4,128)S(1)} collective-permute-done((f32[4,128]{1,0:T(4,128)S(1)}, f32[4,128]{1,0:T(4,128)S(1)}, u32[]{:S(2)}, u32[]{:S(2)}) %collective-permute-start.6) | collective-permute-done | bytes 2080 | tf_op jit(solution)/shard_map/ppermute | solution.py:324
  20.6 0.6 %shard_map.69 = f32[4,64]{1,0:T(4,128)} custom-call(f32[4,128]{1,0:T(4,128)S(1)} %get-tuple-element.23.keep_ref, f32[4,128]{1,0:T(4,128)S(1)} %collective-permute-done.6.got_ref), custom_call_target="tpu_custom_call" | custom-call | tf_op jit(solution)/shard_map/pallas_call | solution.py:314
Async XLA Ops:
  3.0 1.7 %collective-permute-start = (bf16[304,512]{1,0:T(8,128)(2,1)S(1)}, bf16[304,512]{1,0:T(8,128)(2,1)S(1)}, u32[]{:S(2)}, u32[]{:S(2)}) collective-permute-start(bf16[304,512]{1,0:T(8,128)(2,1)S(1)} %get-tuple-element.20), channel_id=1, source_target_pairs={{0,1},{1,0},{2,3},{3,2},{4,5},{5,4},{6,7},{7,6},{8,9},{9,8},{10,11... | collective-permute-start | bytes 933896 | tf_op jit(solution)/shard_map/ppermute | solution.py:324
  5.2 7.3 %collective-permute-start.4 = (bf16[128,256]{1,0:T(8,128)(2,1)S(1)}, bf16[128,256]{1,0:T(8,128)(2,1)S(1)}, u32[]{:S(2)}, u32[]{:S(2)}) collective-permute-start(bf16[128,256]{1,0:T(8,128)(2,1)S(1)} %shard_map.66.refs_0_), channel_id=1, source_target_pairs={{0,13},{1,12},{2,15},{3,14},{4,9},{5,8},{6,11},{7,10},{8,5},{9,4},... | collective-permute-start | bytes 196616 | tf_op jit(solution)/shard_map/ppermute | solution.py:337
  9.9 6.0 %collective-permute-start.3 = (bf16[128,256]{1,0:T(8,128)(2,1)S(1)}, bf16[128,256]{1,0:T(8,128)(2,1)S(1)}, u32[]{:S(2)}, u32[]{:S(2)}) collective-permute-start(bf16[128,256]{1,0:T(8,128)(2,1)S(1)} %shard_map.66.refs_0_), channel_id=1, source_target_pairs={{0,9},{1,8},{2,11},{3,10},{4,13},{5,12},{6,15},{7,14},{8,1},{9,0},... | collective-permute-start | bytes 196616 | tf_op jit(solution)/shard_map/ppermute | solution.py:337
  9.9 6.0 %collective-permute-start.2 = (bf16[128,256]{1,0:T(8,128)(2,1)S(1)}, bf16[128,256]{1,0:T(8,128)(2,1)S(1)}, u32[]{:S(2)}, u32[]{:S(2)}) collective-permute-start(bf16[128,256]{1,0:T(8,128)(2,1)S(1)} %shard_map.66.refs_0_), channel_id=1, source_target_pairs={{0,4},{1,5},{2,6},{3,7},{4,0},{5,1},{6,2},{7,3},{8,12},{9,13},{10,... | collective-permute-start | bytes 196616 | tf_op jit(solution)/shard_map/ppermute | solution.py:337
  10.6 5.3 %collective-permute-start.1 = (bf16[128,256]{1,0:T(8,128)(2,1)S(1)}, bf16[128,256]{1,0:T(8,128)(2,1)S(1)}, u32[]{:S(2)}, u32[]{:S(2)}) collective-permute-start(bf16[128,256]{1,0:T(8,128)(2,1)S(1)} %shard_map.66.refs_0_), channel_id=1, source_target_pairs={{0,2},{2,0},{1,3},{3,1},{4,6},{6,4},{5,7},{7,5},{8,10},{10,8},{9,1... | collective-permute-start | bytes 196616 | tf_op jit(solution)/shard_map/ppermute | solution.py:332
  16.4 3.1 %collective-permute-start.5 = (f32[8,128]{1,0:T(8,128)S(1)}, f32[8,128]{1,0:T(8,128)S(1)}, u32[]{:S(2)}, u32[]{:S(2)}) collective-permute-start(f32[8,128]{1,0:T(8,128)S(1)} %get-tuple-element.22), channel_id=1, source_target_pairs={{0,3},{1,2},{2,1},{3,0},{4,7},{5,6},{6,5},{7,4},{8,11},{9,10},{10,... | collective-permute-start | bytes 12296 | tf_op jit(solution)/shard_map/ppermute | solution.py:328
  19.5 1.2 %collective-permute-start.6 = (f32[4,128]{1,0:T(4,128)S(1)}, f32[4,128]{1,0:T(4,128)S(1)}, u32[]{:S(2)}, u32[]{:S(2)}) collective-permute-start(f32[4,128]{1,0:T(4,128)S(1)} %get-tuple-element.24), channel_id=1, source_target_pairs={{0,1},{1,0},{2,3},{3,2},{4,5},{5,4},{6,7},{7,6},{8,9},{9,8},{10,11... | collective-permute-start | bytes 6152 | tf_op jit(solution)/shard_map/ppermute | solution.py:324

commit v8 on v7

--- a/solution.py
+++ b/solution.py
@@ -156,10 +156,12 @@
             near_waits[1 + ends.index(col)].wait()
         term = lax.dot_general(left, far[:, part], NT, preferred_element_type=F32)
         total = term if total is None else total + term
-        term = lax.dot_general(
-            near_factor[:, part], near_ref[:, part], NT, preferred_element_type=F32
-        )
-        ranks = term if ranks is None else ranks + term
+        if col + wide in ends[-2:]:
+            part = slice(0 if ranks is None else ends[-2], col + wide)
+            term = lax.dot_general(
+                near_factor[:, part], near_ref[:, part], NT, preferred_element_type=F32
+            )
+            ranks = term if ranks is None else ranks + term
     total = jnp.where(far_kept, total, 0.0)
     send_ref[:PROJ_ROWS] = total[:PROJ_ROWS].astype(BF16)
     ranks_ref[...] = split_pieces(total[PROJ_ROWS:])

time: 21.4 us -> 21.7 us (1.014)
  Pallas kernels: 5.53 us -> 5.86 us
    pallas_call x1, Pallas kernels: 3.02 us -> 3.36 us  [far_rows(): pl.pallas_call(functools.partial(far_kernel, cross, ex_rows), out_shape=[...]
where the time goes in v8:
time: 21.7 us; the launch traced here: 21.6 us
  starting transfers between devices  8.95 us (41%)
  waiting for transfers between devices  6.72 us (31%)
  Pallas kernels  5.86 us (27%)
    ppermute x3, starting transfers between devices, swap_z(): lax.ppermute(value, BLK + ('tensor',), [(i, i ^ other) for i in range(16)])  5.43 us
    ppermute x3, waiting for transfers between devices, swap_z(): lax.ppermute(value, BLK + ('tensor',), [(i, i ^ other) for i in range(16)])  3.7 us
    pallas_call x1, Pallas kernels, far_rows(): pl.pallas_call(functools.partial(far_kernel, cross, ex_rows), out_shape=[...  3.36 us
    ppermute x1, waiting for transfers between devices, swap_across(): return lax.ppermute(value, ('x', 'tensor'), [(i, i ^ 3) for i in range(4)])  1.79 us
    ppermute x1, starting transfers between devices, swap_x(): return lax.ppermute(value, 'x', [(0, 1), (1, 0)])  1.6 us
    ppermute x1, starting transfers between devices, swap_across(): return lax.ppermute(value, ('x', 'tensor'), [(i, i ^ 3) for i in range(4)])  1.26 us
    ppermute x2, waiting for transfers between devices, swap_cores(): return lax.ppermute(value, 'tensor', [(0, 1), (1, 0)])  1.23 us
    pallas_call x1, Pallas kernels, near_rows(): pl.pallas_call(near_kernel, out_shape=jax.ShapeDtypeStruct((PROJ_ROWS, to...  1.02 us
  transfers between devices with their start and end apart: 7, of which 5 were waited for; matrix products, arithmetic and copies ran while one was open for 0% of the time, Pallas kernels for 5%

profile of v8, /device:TPU:0, one launch (start us, length us, event | category | flops | bytes accessed | tf_op | source)
XLA Modules:
  0.0 21.6 jit_solution(17527917462068061109)
XLA Ops:
  0.0 3.4 %shard_map.64 = (bf16[304,512]{1,0:T(8,128)(2,1)S(1)}, bf16[48,512]{1,0:T(8,128)(2,1)S(1)}, bf16[512,2048]{1,0:T(8,128)(2,1)S(1)}, s32[16,256]{1,0:T(8,128)S(1)}...) custom-call(s32[4]{0:T(128)} %salts_hbm.1, s32[8,64]{1,0:T(8,128)} %mask_hbm.1, bf16[16,2048]{1,0:T(8,128)(2,1)} %down_hbm.1, ...), custom_call_target="tpu_custom_call" | custom-call | tf_op jit(solution)/shard_map/pallas_call | solution.py:176
  3.4 0.5 %collective-permute-start = (bf16[304,512]{1,0:T(8,128)(2,1)S(1)}, bf16[304,512]{1,0:T(8,128)(2,1)S(1)}, u32[]{:S(2)}, u32[]{:S(2)}) collective-permute-start(bf16[304,512]{1,0:T(8,128)(2,1)S(1)} %get-tuple-element.20), channel_id=1, source_target_pairs={{0,1},{1,0},{2,3},{3,2},{4,5},{5,4},{6,7},{7,6},{8,9},{9,8},{10,11... | collective-permute-start | bytes 933896 | tf_op jit(solution)/shard_map/ppermute | solution.py:326
  3.9 1.0 %shard_map.65.own_ref = bf16[256,512]{1,0:T(8,128)(2,1)S(1)} custom-call(s32[16,256]{1,0:T(8,128)S(1)} %get-tuple-element.17.start_ref, f32[8,512]{1,0:T(8,128)S(1)} %get-tuple-element.18.kept_ref, bf16[512,2048]{1,0:T(8,128)(2,1)S(1)} %get-tuple-element.19.near_ref), custom_call_target="tpu_custom_call" | custom-call | flops 536870912 | bytes 2097152 | tf_op jit(solution)/shard_map/pallas_call | solution.py:215
  4.9 0.2 collective-permute-done.other_ref
  5.1 0.4 %shard_map.66.refs_0_ = bf16[128,256]{1,0:T(8,128)(2,1)S(1)} custom-call(bf16[128,96]{1,0:T(8,128)(2,1)S(1)} %get-tuple-element.15.mixer_ref, bf16[48,512]{1,0:T(8,128)(2,1)S(1)} %get-tuple-element.16.ranks_ref, bf16[256,512]{1,0:T(8,128)(2,1)S(1)} %shard_map.65.own_ref, bf16[304,512]{1,0:T(8,128)(2,1)S(1)} %collective-permute-done.other_ref), custom_call_target="tpu_custom_call" | custom-call | tf_op jit(solution)/shard_map/pallas_call | solution.py:240
  5.5 4.8 %collective-permute-start.4 = (bf16[128,256]{1,0:T(8,128)(2,1)S(1)}, bf16[128,256]{1,0:T(8,128)(2,1)S(1)}, u32[]{:S(2)}, u32[]{:S(2)}) collective-permute-start(bf16[128,256]{1,0:T(8,128)(2,1)S(1)} %shard_map.66.refs_0_), channel_id=1, source_target_pairs={{0,13},{1,12},{2,15},{3,14},{4,9},{5,8},{6,11},{7,10},{8,5},{9,4},... | collective-permute-start | bytes 196616 | tf_op jit(solution)/shard_map/ppermute | solution.py:339
  10.3 0.0 collective-permute-start.3
  10.3 0.7 %collective-permute-start.2 = (bf16[128,256]{1,0:T(8,128)(2,1)S(1)}, bf16[128,256]{1,0:T(8,128)(2,1)S(1)}, u32[]{:S(2)}, u32[]{:S(2)}) collective-permute-start(bf16[128,256]{1,0:T(8,128)(2,1)S(1)} %shard_map.66.refs_0_), channel_id=1, source_target_pairs={{0,4},{1,5},{2,6},{3,7},{4,0},{5,1},{6,2},{7,3},{8,12},{9,13},{10,... | collective-permute-start | bytes 196616 | tf_op jit(solution)/shard_map/ppermute | solution.py:339
  10.9 1.6 %collective-permute-start.1 = (bf16[128,256]{1,0:T(8,128)(2,1)S(1)}, bf16[128,256]{1,0:T(8,128)(2,1)S(1)}, u32[]{:S(2)}, u32[]{:S(2)}) collective-permute-start(bf16[128,256]{1,0:T(8,128)(2,1)S(1)} %shard_map.66.refs_0_), channel_id=1, source_target_pairs={{0,2},{2,0},{1,3},{3,1},{4,6},{6,4},{5,7},{7,5},{8,10},{10,8},{9,1... | collective-permute-start | bytes 196616 | tf_op jit(solution)/shard_map/ppermute | solution.py:334
  12.5 0.3 %collective-permute-done.4.refs_3_ = bf16[128,256]{1,0:T(8,128)(2,1)S(1)} collective-permute-done((bf16[128,256]{1,0:T(8,128)(2,1)S(1)}, bf16[128,256]{1,0:T(8,128)(2,1)S(1)}, u32[]{:S(2)}, u32[]{:S(2)}) %collective-permute-start.4) | collective-permute-done | bytes 65568 | tf_op jit(solution)/shard_map/ppermute | solution.py:339
  12.8 3.4 %collective-permute-done.3.refs_2_ = bf16[128,256]{1,0:T(8,128)(2,1)S(1)} collective-permute-done((bf16[128,256]{1,0:T(8,128)(2,1)S(1)}, bf16[128,256]{1,0:T(8,128)(2,1)S(1)}, u32[]{:S(2)}, u32[]{:S(2)}) %collective-permute-start.3) | collective-permute-done | bytes 65568 | tf_op jit(solution)/shard_map/ppermute | solution.py:339
  16.2 0.0 collective-permute-done.2.refs_1_
  16.2 0.0 collective-permute-done.1.near_ref
  16.2 0.5 %shard_map.67 = (f32[8,128]{1,0:T(8,128)S(1)}, f32[8,128]{1,0:T(8,128)S(1)}) custom-call(bf16[128,256]{1,0:T(8,128)(2,1)S(1)} %collective-permute-done.1.near_ref, bf16[128,256]{1,0:T(8,128)(2,1)S(1)} %shard_map.66.refs_0_, bf16[128,256]{1,0:T(8,128)(2,1)S(1)} %collective-permute-done.2.refs_1_, bf16[128,256]{1,0:T(8,128)(2,1)S(1)} %collective-permute-done.3.refs_2_, ...), custom_call_target="tpu_custom_call" | custom-call | tf_op jit(solution)/shard_map/pallas_call | solution.py:279
  16.7 1.3 %collective-permute-start.5 = (f32[8,128]{1,0:T(8,128)S(1)}, f32[8,128]{1,0:T(8,128)S(1)}, u32[]{:S(2)}, u32[]{:S(2)}) collective-permute-start(f32[8,128]{1,0:T(8,128)S(1)} %get-tuple-element.22), channel_id=1, source_target_pairs={{0,3},{1,2},{2,1},{3,0},{4,7},{5,6},{6,5},{7,4},{8,11},{9,10},{10,... | collective-permute-start | bytes 12296 | tf_op jit(solution)/shard_map/ppermute | solution.py:330
  18.0 1.8 %collective-permute-done.5.got_ref = f32[8,128]{1,0:T(8,128)S(1)} collective-permute-done((f32[8,128]{1,0:T(8,128)S(1)}, f32[8,128]{1,0:T(8,128)S(1)}, u32[]{:S(2)}, u32[]{:S(2)}) %collective-permute-start.5) | collective-permute-done | bytes 4128 | tf_op jit(solution)/shard_map/ppermute | solution.py:330
  19.7 0.1 shard_map.68
  19.8 0.1 collective-permute-start.6
  20.0 1.0 %collective-permute-done.6.got_ref = f32[4,128]{1,0:T(4,128)S(1)} collective-permute-done((f32[4,128]{1,0:T(4,128)S(1)}, f32[4,128]{1,0:T(4,128)S(1)}, u32[]{:S(2)}, u32[]{:S(2)}) %collective-permute-start.6) | collective-permute-done | bytes 2080 | tf_op jit(solution)/shard_map/ppermute | solution.py:326
  21.0 0.6 %shard_map.69 = f32[4,64]{1,0:T(4,128)} custom-call(f32[4,128]{1,0:T(4,128)S(1)} %get-tuple-element.23.keep_ref, f32[4,128]{1,0:T(4,128)S(1)} %collective-permute-done.6.got_ref), custom_call_target="tpu_custom_call" | custom-call | tf_op jit(solution)/shard_map/pallas_call | solution.py:316
Async XLA Ops:
  3.4 1.7 %collective-permute-start = (bf16[304,512]{1,0:T(8,128)(2,1)S(1)}, bf16[304,512]{1,0:T(8,128)(2,1)S(1)}, u32[]{:S(2)}, u32[]{:S(2)}) collective-permute-start(bf16[304,512]{1,0:T(8,128)(2,1)S(1)} %get-tuple-element.20), channel_id=1, source_target_pairs={{0,1},{1,0},{2,3},{3,2},{4,5},{5,4},{6,7},{7,6},{8,9},{9,8},{10,11... | collective-permute-start | bytes 933896 | tf_op jit(solution)/shard_map/ppermute | solution.py:326
  5.5 7.3 %collective-permute-start.4 = (bf16[128,256]{1,0:T(8,128)(2,1)S(1)}, bf16[128,256]{1,0:T(8,128)(2,1)S(1)}, u32[]{:S(2)}, u32[]{:S(2)}) collective-permute-start(bf16[128,256]{1,0:T(8,128)(2,1)S(1)} %shard_map.66.refs_0_), channel_id=1, source_target_pairs={{0,13},{1,12},{2,15},{3,14},{4,9},{5,8},{6,11},{7,10},{8,5},{9,4},... | collective-permute-start | bytes 196616 | tf_op jit(solution)/shard_map/ppermute | solution.py:339
  10.3 6.0 %collective-permute-start.3 = (bf16[128,256]{1,0:T(8,128)(2,1)S(1)}, bf16[128,256]{1,0:T(8,128)(2,1)S(1)}, u32[]{:S(2)}, u32[]{:S(2)}) collective-permute-start(bf16[128,256]{1,0:T(8,128)(2,1)S(1)} %shard_map.66.refs_0_), channel_id=1, source_target_pairs={{0,9},{1,8},{2,11},{3,10},{4,13},{5,12},{6,15},{7,14},{8,1},{9,0},... | collective-permute-start | bytes 196616 | tf_op jit(solution)/shard_map/ppermute | solution.py:339
  10.3 6.0 %collective-permute-start.2 = (bf16[128,256]{1,0:T(8,128)(2,1)S(1)}, bf16[128,256]{1,0:T(8,128)(2,1)S(1)}, u32[]{:S(2)}, u32[]{:S(2)}) collective-permute-start(bf16[128,256]{1,0:T(8,128)(2,1)S(1)} %shard_map.66.refs_0_), channel_id=1, source_target_pairs={{0,4},{1,5},{2,6},{3,7},{4,0},{5,1},{6,2},{7,3},{8,12},{9,13},{10,... | collective-permute-start | bytes 196616 | tf_op jit(solution)/shard_map/ppermute | solution.py:339
  10.9 5.3 %collective-permute-start.1 = (bf16[128,256]{1,0:T(8,128)(2,1)S(1)}, bf16[128,256]{1,0:T(8,128)(2,1)S(1)}, u32[]{:S(2)}, u32[]{:S(2)}) collective-permute-start(bf16[128,256]{1,0:T(8,128)(2,1)S(1)} %shard_map.66.refs_0_), channel_id=1, source_target_pairs={{0,2},{2,0},{1,3},{3,1},{4,6},{6,4},{5,7},{7,5},{8,10},{10,8},{9,1... | collective-permute-start | bytes 196616 | tf_op jit(solution)/shard_map/ppermute | solution.py:334
  16.7 3.1 %collective-permute-start.5 = (f32[8,128]{1,0:T(8,128)S(1)}, f32[8,128]{1,0:T(8,128)S(1)}, u32[]{:S(2)}, u32[]{:S(2)}) collective-permute-start(f32[8,128]{1,0:T(8,128)S(1)} %get-tuple-element.22), channel_id=1, source_target_pairs={{0,3},{1,2},{2,1},{3,0},{4,7},{5,6},{6,5},{7,4},{8,11},{9,10},{10,... | collective-permute-start | bytes 12296 | tf_op jit(solution)/shard_map/ppermute | solution.py:330
  19.8 1.2 %collective-permute-start.6 = (f32[4,128]{1,0:T(4,128)S(1)}, f32[4,128]{1,0:T(4,128)S(1)}, u32[]{:S(2)}, u32[]{:S(2)}) collective-permute-start(f32[4,128]{1,0:T(4,128)S(1)} %get-tuple-element.24), channel_id=1, source_target_pairs={{0,1},{1,0},{2,3},{3,2},{4,5},{5,4},{6,7},{7,6},{8,9},{9,8},{10,11... | collective-permute-start | bytes 6152 | tf_op jit(solution)/shard_map/ppermute | solution.py:326
